TPU v7x, 32 devices: a whole 2x2x4 slice. The times are simulated.
32 devices in a mesh: gx: 8 (over y, x, core), gy: 4 (over z).
Axes of the slice: x: 2, y: 2, z: 4, core: 2. Of those that a mesh axis runs over, the one named last changes fastest.
Arguments:
- thermal_anomaly_grid: float32 [30, 128, 1024], P(None, 'gy', 'gx'), may hold values from -5 to 5
- relative_moisture: float32 [30, 128, 1024], P(None, 'gy', 'gx'), may hold values from 0.05 to 1
- overcast_share: float32 [30, 128, 1024], P(None, 'gy', 'gx'), may hold values from 0 to 1
- sun_angle_projection: float32 [128, 1024], P('gy', 'gx'), may hold values from 0.1 to 1
- daylight_mask: int32 [8, 128], P('gx', 'gy'), may hold values 0 or 1
- radiator_owner_position: int32 [8, 128, 1], P('gx', 'gy'), may hold values from 0 to 7; in each aligned block of 32 rows (0 to 31, 32 to 63, ..., all dimensions but the last counted through in order) at most 8 rows name the same one
- molecular_opacity_lookup: bfloat16 [30, 140, 128], replicated, may hold values from 0.019897461 to 1.5
- condensed_opacity_per_share: float32 [140], replicated, may hold values from 0.05 to 1
- planck_emission_factor: float32 [140], replicated, may hold values from 0.2 to 1
- insolation_quadrature_factor: float32 [140], replicated, may hold values from 0.2 to 2
Outputs:
- advanced_anomaly_grid: float32 [30, 128, 1024], P(None, 'gy', 'gx')
- humidity_next: float32 [30, 128, 1024], P(None, 'gy', 'gx')
- ground_irradiance_slots: float32 [4, 8, 8, 8, 128], P('gy', 'gx')
Inputs may be any that keep to these rules, and one draw needn't show every extreme that they name: `radiator_owner_position`: among the 32 blocks of one device, at most 8 name the same host, and some device's blocks name one host exactly 8 times.
All inputs are finite; a program needn't handle non-finite values. No bound on the sum of `daylight_mask` on one device may be relied on, other than what follows from the above.
Results may differ from a plain program's by a relative error of at most 0.0034.
Values may be sent and summed in bfloat16 or wider, within the bound.
No kernel may reach another device: no remote copies, remote signals or barrier semaphores. Data moves between devices by JAX's collectives and lax.ppermute only.
A program may use at most 128 MiB of HBM per device.

v0:
```python
import jax
import jax.numpy as jnp
from jax import lax
from jax.sharding import PartitionSpec as P

NT = 16
NQ = 8


diffusion = 0.2
diffusivity = 1.66


def extended(block, sides, width):
    for axis, dim in sides:
        count = lax.axis_size(axis)
        forward = [(i, i + 1) for i in range(count - 1)]
        backward = [(target, source) for source, target in forward]
        low = lax.ppermute(
            lax.slice_in_dim(block, block.shape[dim] - width, None, axis=dim), axis, forward
        )
        high = lax.ppermute(lax.slice_in_dim(block, 0, width, axis=dim), axis, backward)
        block = jnp.concatenate([low, block, high], axis=dim)
    return block


def stencil(bordered_grid):
    centre = bordered_grid[:, :, 1:-1, 1:-1]
    beside_all = (
        bordered_grid[:, :, 2:, 1:-1]
        + bordered_grid[:, :, :-2, 1:-1]
        + bordered_grid[:, :, 1:-1, 2:]
        + bordered_grid[:, :, 1:-1, :-2]
    )
    return centre + diffusion * (beside_all - 4.0 * centre)


def optical_depth(layer, table_layer, condensed_opacity_per_share):
    air_temp, moisture, condensate = (layer[0], layer[1], layer[2])
    temp_nodes = jnp.arange(NT, dtype=jnp.float32)
    humid_nodes = jnp.arange(NQ, dtype=jnp.float32)
    temp_pos = jnp.clip((air_temp + 3.0) * ((NT - 1.0) / 6.0), 0.0, NT - 1.0)
    humid_pos = jnp.clip(moisture * (NQ - 1.0), 0.0, NQ - 1.0)
    temp_hat = jnp.maximum(0.0, 1.0 - jnp.abs(temp_pos[None, :] - temp_nodes[:, None]))
    humid_hat = jnp.maximum(0.0, 1.0 - jnp.abs(humid_pos[None, :] - humid_nodes[:, None]))
    weights = (
        (temp_hat[:, None, :] * humid_hat[None, :, :]).reshape(NT * NQ, -1).astype(jnp.bfloat16)
    )
    gas_depth = jnp.dot(table_layer, weights, preferred_element_type=jnp.float32)
    return gas_depth + condensed_opacity_per_share[:, None] * condensate[None, :]


def column_physics(
    prognostic_bundle,
    zenith,
    incident,
    molecular_opacity_lookup,
    condensed_opacity_per_share,
    planck_emission_factor,
    insolation_quadrature_factor,
):
    layers = jnp.transpose(prognostic_bundle, (1, 0, 2))
    gpoints = planck_emission_factor.shape[0]

    def downward(carry, inputs):
        long_down, short_down = carry
        layer, table_layer = inputs
        depth = optical_depth(layer, table_layer, condensed_opacity_per_share)
        through = jnp.exp(-diffusivity * depth)
        source = planck_emission_factor[:, None] * (1.0 + 0.25 * layer[0][None, :])
        long_next = long_down * through + (1.0 - through) * source
        short_next = short_down * jnp.exp(-depth / zenith[None, :])
        gained = jnp.sum(long_down - long_next + short_down - short_next, axis=0)
        return ((long_next, short_next), gained)

    def upward(long_up, inputs):
        layer, table_layer = inputs
        depth = optical_depth(layer, table_layer, condensed_opacity_per_share)
        through = jnp.exp(-diffusivity * depth)
        source = planck_emission_factor[:, None] * (1.0 + 0.25 * layer[0][None, :])
        long_next = long_up * through + (1.0 - through) * source
        return (long_next, jnp.sum(long_up - long_next, axis=0))

    start_long = jnp.zeros((gpoints, prognostic_bundle.shape[2]), jnp.float32)
    start_short = insolation_quadrature_factor[:, None] * incident[None, :]
    bottom, down_gain = lax.scan(
        downward, (start_long, start_short), (layers, molecular_opacity_lookup)
    )
    start_up = planck_emission_factor[:, None] * (1.0 + 0.25 * layers[-1, 0][None, :])
    top_up, up_gain = lax.scan(upward, start_up, (layers, molecular_opacity_lookup), reverse=True)
    heating = 2.0 / gpoints * (down_gain + up_gain)
    ground_irradiance_result = jnp.sum(bottom[0] + bottom[1], axis=0) / gpoints
    return (heating, ground_irradiance_result)


def block_rank(hosts):
    profile_groups = hosts.shape[-1]
    earlier = jnp.arange(profile_groups)[None, :] < jnp.arange(profile_groups)[:, None]
    same = hosts[..., :, None] == hosts[..., None, :]
    return jnp.sum(jnp.logical_and(same, earlier), axis=-1)


def slot_table(hosts, host_ids, capacity):
    rank = block_rank(hosts)
    slot_ids = jnp.arange(capacity, dtype=jnp.int32)[None, :, None]
    chosen = jnp.logical_and(
        hosts[..., None, None, :] == host_ids[:, None, None], rank[..., None, None, :] == slot_ids
    )
    return chosen.astype(jnp.float32)


def radiate(
    received_state,
    received_light,
    molecular_opacity_lookup,
    condensed_opacity_per_share,
    planck_emission_factor,
    insolation_quadrature_factor,
):
    sources, items = (received_state.shape[0], received_state.shape[1])
    level_count, width = (received_state.shape[3], received_state.shape[4])
    columns = sources * items * width
    prognostic_bundle = (
        jnp.transpose(received_state, (2, 3, 0, 1, 4))
        .reshape(3, level_count, columns)
        .astype(jnp.float32)
    )
    shine = jnp.transpose(received_light, (2, 0, 1, 3)).reshape(2, columns).astype(jnp.float32)
    occupied = shine[0] > 0.0
    zenith = jnp.where(occupied, shine[0], 1.0)
    heating, ground_irradiance_result = column_physics(
        prognostic_bundle,
        zenith,
        shine[1],
        molecular_opacity_lookup,
        condensed_opacity_per_share,
        planck_emission_factor,
        insolation_quadrature_factor,
    )
    ground_irradiance_result = jnp.where(occupied, ground_irradiance_result, 0.0)
    heating = jnp.transpose(heating.reshape(level_count, sources, items, width), (1, 2, 0, 3))
    return (heating, ground_irradiance_result.reshape(sources, items, width))


def on_device(
    thermal_anomaly_grid,
    relative_moisture,
    overcast_share,
    sun_angle_projection,
    daylight_mask,
    radiator_owner_position,
    molecular_opacity_lookup,
    condensed_opacity_per_share,
    planck_emission_factor,
    insolation_quadrature_factor,
):
    host_count = lax.axis_size("gx")
    profile_groups = thermal_anomaly_grid.shape[1]
    capacity = max(2, (2 * profile_groups + host_count - 1) // host_count)
    bordered_grid = extended(
        jnp.stack((thermal_anomaly_grid, relative_moisture)), (("gx", 3), ("gy", 2)), 1
    )
    laplacian_blurred_grid = stencil(bordered_grid)
    prognostic_bundle = jnp.stack((thermal_anomaly_grid, relative_moisture, overcast_share)).astype(
        jnp.bfloat16
    )
    lit_rows = daylight_mask[0].astype(jnp.float32)[:, None]
    light = jnp.stack((sun_angle_projection, sun_angle_projection * lit_rows)).astype(jnp.bfloat16)
    own_hosts = radiator_owner_position[0, :, 0]
    slot_position = own_hosts * capacity + block_rank(own_hosts)
    every_state, every_light, every_host = (
        lax.all_gather(prognostic_bundle[None], "gx", axis=0, tiled=True),
        lax.all_gather(light[None], "gx", axis=0, tiled=True),
        lax.all_gather(own_hosts[None], "gx", axis=0, tiled=True),
    )
    mine = jnp.reshape(lax.axis_index("gx"), (1,))
    chooser = slot_table(every_host, mine, capacity)[:, 0].astype(jnp.bfloat16)
    received_state = jnp.einsum(
        "skb,sclbx->skclx", chooser, every_state, preferred_element_type=jnp.float32
    ).astype(jnp.bfloat16)
    received_light = jnp.einsum(
        "skb,scbx->skcx", chooser, every_light, preferred_element_type=jnp.float32
    ).astype(jnp.bfloat16)
    heating, ground_irradiance_result = radiate(
        received_state,
        received_light,
        molecular_opacity_lookup,
        condensed_opacity_per_share,
        planck_emission_factor,
        insolation_quadrature_factor,
    )
    returned = lax.all_to_all(heating, "gx", split_axis=0, concat_axis=0, tiled=True)
    flat_returned = returned.reshape(
        returned.shape[0] * returned.shape[1], returned.shape[2], returned.shape[3]
    )
    own_warming_rates = jnp.transpose(flat_returned[slot_position], (1, 0, 2))
    advanced_anomaly_grid = laplacian_blurred_grid[0] + own_warming_rates
    return (advanced_anomaly_grid, laplacian_blurred_grid[1], ground_irradiance_result[None, None])


def solution(mesh):
    placed = (
        P(None, "gy", "gx"),
        P(None, "gy", "gx"),
        P(None, "gy", "gx"),
        P("gy", "gx"),
        P("gx", "gy"),
        P("gx", "gy", None),
        P(),
        P(),
        P(),
        P(),
    )
    return jax.shard_map(
        on_device,
        mesh=mesh,
        in_specs=placed,
        out_specs=(P(None, "gy", "gx"), P(None, "gy", "gx"), P("gy", "gx", None, None, None)),
        check_vma=False,
    )
```

profile of v0, /device:TPU:20, one launch (start us, length us, event | category | flops | bytes accessed | tf_op | source)
XLA Modules:
  0.0 610.8 jit_solution(10304782899113299827)
XLA Ops:
  19.5 7.8 %all-gather = s32[8,32,1]{1,2,0:T(1,128)S(1)} all-gather(s32[1,32,1]{1,2,0:T(1,128)S(1)} %copy-done.6), channel_id=2, replica_groups=mesh['gx'=8,'gy'=4] {'gx'}, dimensions={0}, use_global_device_ids=true | all-gather | bytes 1152 | tf_op jit(solution)/shard_map/all_gather | solution.py:174
  27.4 9.1 %all_gather.10 = bf16[8,2,32,128]{3,2,1,0:T(8,128)(2,1)S(1)} all-gather(bf16[1,2,32,128]{3,2,1,0:T(8,128)(2,1)S(1)} %pad_maximum_fusion.18), channel_id=1, replica_groups=mesh['gx'=8,'gy'=4] {'gx'}, dimensions={0}, use_global_device_ids=true | all-gather | bytes 147456 | tf_op jit(solution)/shard_map/all_gather | solution.py:173
  70.4 217.4 %while.31 = (s32[]{:T(128)}, f32[140,8192]{1,0:T(8,128)}, f32[30,8192]{1,0:T(8,128)S(1)}, bf16[30,140,128]{2,1,0:T(8,128)(2,1)}, f32[30,3,8192]{2,1,0:T(4,128)},...) while((s32[]{:T(128)}, f32[140,8192]{1,0:T(8,128)}, ...), condition=%wide.region_6.7_spmd, body=%wide.region_4.6_spmd.sunk | while | flops 308002816 | bytes 11375885 | solution.py:90
  79.0 5.7 subtract_reduce_fusion.4
  86.3 5.7 subtract_reduce_fusion.4
  93.5 5.7 subtract_reduce_fusion.4
  158.7 5.7 subtract_reduce_fusion.4
  166.0 5.7 subtract_reduce_fusion.4
  173.2 5.7 subtract_reduce_fusion.4
  180.5 5.7 subtract_reduce_fusion.4
  195.0 5.7 subtract_reduce_fusion.4
  202.2 5.7 subtract_reduce_fusion.4
  216.7 5.7 subtract_reduce_fusion.4
  224.0 5.7 subtract_reduce_fusion.4
  245.7 5.7 subtract_reduce_fusion.4
  252.9 5.7 subtract_reduce_fusion.4
  287.9 295.1 %while.32 = (s32[]{:T(128)}, f32[140,8192]{1,0:T(8,128)}, f32[140,8192]{1,0:T(8,128)}, f32[30,8192]{1,0:T(8,128)S(1)}, bf16[30,140,128]{2,1,0:T(8,128)(2,1)}, /*...) while((s32[]{:T(128)}, f32[140,8192]{1,0:T(8,128)}, ...), condition=%wide.region_3.4_spmd.clone, body=%wide.region_1.3_spmd.clone.sunk | while | flops 314884096 | bytes 20714776 | solution.py:86
  289.3 7.6 %subtract_reduce_fusion.5 = (f32[8192]{0:T(1024)S(1)}, f32[140,8192]{1,0:T(8,128)}, f32[140,8192]{1,0:T(8,128)}) fusion(f32[140,8192]{1,0:T(8,128)} %get-tuple-element.497, f32[140,8192]{1,0:T(8,128)} %get-tuple-element.496, pred[]{:T(512)S(6)} %compare.3, f32[8192]{0:T(1024)S(1)} %get-tuple-element.516, f32[8192]{0:T(1024)S(1)} %bitcast.137, ...), kind=kOutput, calls=%fused_computation.21.clone.1 | convolution fusion | flops 314040320 | bytes 19567716 | tf_op jit(solution)/shard_map/while/body/eval_jaxpr/dot_general | solution.py:49
  298.4 8.4 %subtract_reduce_fusion.5 = (f32[8192]{0:T(1024)S(1)}, f32[140,8192]{1,0:T(8,128)}, f32[140,8192]{1,0:T(8,128)}) fusion(f32[140,8192]{1,0:T(8,128)} %get-tuple-element.497, f32[140,8192]{1,0:T(8,128)} %get-tuple-element.496, pred[]{:T(512)S(6)} %compare.3, f32[8192]{0:T(1024)S(1)} %get-tuple-element.516, f32[8192]{0:T(1024)S(1)} %bitcast.137, ...), kind=kOutput, calls=%fused_computation.21.clone.1 | convolution fusion | flops 314040320 | bytes 19567716 | tf_op jit(solution)/shard_map/while/body/eval_jaxpr/dot_general | solution.py:49
  308.3 8.4 %subtract_reduce_fusion.5 = (f32[8192]{0:T(1024)S(1)}, f32[140,8192]{1,0:T(8,128)}, f32[140,8192]{1,0:T(8,128)}) fusion(f32[140,8192]{1,0:T(8,128)} %get-tuple-element.497, f32[140,8192]{1,0:T(8,128)} %get-tuple-element.496, pred[]{:T(512)S(6)} %compare.3, f32[8192]{0:T(1024)S(1)} %get-tuple-element.516, f32[8192]{0:T(1024)S(1)} %bitcast.137, ...), kind=kOutput, calls=%fused_computation.21.clone.1 | convolution fusion | flops 314040320 | bytes 19567716 | tf_op jit(solution)/shard_map/while/body/eval_jaxpr/dot_general | solution.py:49
  318.2 8.4 %subtract_reduce_fusion.5 = (f32[8192]{0:T(1024)S(1)}, f32[140,8192]{1,0:T(8,128)}, f32[140,8192]{1,0:T(8,128)}) fusion(f32[140,8192]{1,0:T(8,128)} %get-tuple-element.497, f32[140,8192]{1,0:T(8,128)} %get-tuple-element.496, pred[]{:T(512)S(6)} %compare.3, f32[8192]{0:T(1024)S(1)} %get-tuple-element.516, f32[8192]{0:T(1024)S(1)} %bitcast.137, ...), kind=kOutput, calls=%fused_computation.21.clone.1 | convolution fusion | flops 314040320 | bytes 19567716 | tf_op jit(solution)/shard_map/while/body/eval_jaxpr/dot_general | solution.py:49
  328.0 8.4 %subtract_reduce_fusion.5 = (f32[8192]{0:T(1024)S(1)}, f32[140,8192]{1,0:T(8,128)}, f32[140,8192]{1,0:T(8,128)}) fusion(f32[140,8192]{1,0:T(8,128)} %get-tuple-element.497, f32[140,8192]{1,0:T(8,128)} %get-tuple-element.496, pred[]{:T(512)S(6)} %compare.3, f32[8192]{0:T(1024)S(1)} %get-tuple-element.516, f32[8192]{0:T(1024)S(1)} %bitcast.137, ...), kind=kOutput, calls=%fused_computation.21.clone.1 | convolution fusion | flops 314040320 | bytes 19567716 | tf_op jit(solution)/shard_map/while/body/eval_jaxpr/dot_general | solution.py:49
  337.9 8.4 %subtract_reduce_fusion.5 = (f32[8192]{0:T(1024)S(1)}, f32[140,8192]{1,0:T(8,128)}, f32[140,8192]{1,0:T(8,128)}) fusion(f32[140,8192]{1,0:T(8,128)} %get-tuple-element.497, f32[140,8192]{1,0:T(8,128)} %get-tuple-element.496, pred[]{:T(512)S(6)} %compare.3, f32[8192]{0:T(1024)S(1)} %get-tuple-element.516, f32[8192]{0:T(1024)S(1)} %bitcast.137, ...), kind=kOutput, calls=%fused_computation.21.clone.1 | convolution fusion | flops 314040320 | bytes 19567716 | tf_op jit(solution)/shard_map/while/body/eval_jaxpr/dot_general | solution.py:49
  347.7 8.4 %subtract_reduce_fusion.5 = (f32[8192]{0:T(1024)S(1)}, f32[140,8192]{1,0:T(8,128)}, f32[140,8192]{1,0:T(8,128)}) fusion(f32[140,8192]{1,0:T(8,128)} %get-tuple-element.497, f32[140,8192]{1,0:T(8,128)} %get-tuple-element.496, pred[]{:T(512)S(6)} %compare.3, f32[8192]{0:T(1024)S(1)} %get-tuple-element.516, f32[8192]{0:T(1024)S(1)} %bitcast.137, ...), kind=kOutput, calls=%fused_computation.21.clone.1 | convolution fusion | flops 314040320 | bytes 19567716 | tf_op jit(solution)/shard_map/while/body/eval_jaxpr/dot_general | solution.py:49
  357.6 8.4 %subtract_reduce_fusion.5 = (f32[8192]{0:T(1024)S(1)}, f32[140,8192]{1,0:T(8,128)}, f32[140,8192]{1,0:T(8,128)}) fusion(f32[140,8192]{1,0:T(8,128)} %get-tuple-element.497, f32[140,8192]{1,0:T(8,128)} %get-tuple-element.496, pred[]{:T(512)S(6)} %compare.3, f32[8192]{0:T(1024)S(1)} %get-tuple-element.516, f32[8192]{0:T(1024)S(1)} %bitcast.137, ...), kind=kOutput, calls=%fused_computation.21.clone.1 | convolution fusion | flops 314040320 | bytes 19567716 | tf_op jit(solution)/shard_map/while/body/eval_jaxpr/dot_general | solution.py:49
  367.4 8.4 %subtract_reduce_fusion.5 = (f32[8192]{0:T(1024)S(1)}, f32[140,8192]{1,0:T(8,128)}, f32[140,8192]{1,0:T(8,128)}) fusion(f32[140,8192]{1,0:T(8,128)} %get-tuple-element.497, f32[140,8192]{1,0:T(8,128)} %get-tuple-element.496, pred[]{:T(512)S(6)} %compare.3, f32[8192]{0:T(1024)S(1)} %get-tuple-element.516, f32[8192]{0:T(1024)S(1)} %bitcast.137, ...), kind=kOutput, calls=%fused_computation.21.clone.1 | convolution fusion | flops 314040320 | bytes 19567716 | tf_op jit(solution)/shard_map/while/body/eval_jaxpr/dot_general | solution.py:49
  377.3 8.4 %subtract_reduce_fusion.5 = (f32[8192]{0:T(1024)S(1)}, f32[140,8192]{1,0:T(8,128)}, f32[140,8192]{1,0:T(8,128)}) fusion(f32[140,8192]{1,0:T(8,128)} %get-tuple-element.497, f32[140,8192]{1,0:T(8,128)} %get-tuple-element.496, pred[]{:T(512)S(6)} %compare.3, f32[8192]{0:T(1024)S(1)} %get-tuple-element.516, f32[8192]{0:T(1024)S(1)} %bitcast.137, ...), kind=kOutput, calls=%fused_computation.21.clone.1 | convolution fusion | flops 314040320 | bytes 19567716 | tf_op jit(solution)/shard_map/while/body/eval_jaxpr/dot_general | solution.py:49
  387.2 8.4 %subtract_reduce_fusion.5 = (f32[8192]{0:T(1024)S(1)}, f32[140,8192]{1,0:T(8,128)}, f32[140,8192]{1,0:T(8,128)}) fusion(f32[140,8192]{1,0:T(8,128)} %get-tuple-element.497, f32[140,8192]{1,0:T(8,128)} %get-tuple-element.496, pred[]{:T(512)S(6)} %compare.3, f32[8192]{0:T(1024)S(1)} %get-tuple-element.516, f32[8192]{0:T(1024)S(1)} %bitcast.137, ...), kind=kOutput, calls=%fused_computation.21.clone.1 | convolution fusion | flops 314040320 | bytes 19567716 | tf_op jit(solution)/shard_map/while/body/eval_jaxpr/dot_general | solution.py:49
  397.0 8.4 %subtract_reduce_fusion.5 = (f32[8192]{0:T(1024)S(1)}, f32[140,8192]{1,0:T(8,128)}, f32[140,8192]{1,0:T(8,128)}) fusion(f32[140,8192]{1,0:T(8,128)} %get-tuple-element.497, f32[140,8192]{1,0:T(8,128)} %get-tuple-element.496, pred[]{:T(512)S(6)} %compare.3, f32[8192]{0:T(1024)S(1)} %get-tuple-element.516, f32[8192]{0:T(1024)S(1)} %bitcast.137, ...), kind=kOutput, calls=%fused_computation.21.clone.1 | convolution fusion | flops 314040320 | bytes 19567716 | tf_op jit(solution)/shard_map/while/body/eval_jaxpr/dot_general | solution.py:49
  406.9 8.4 %subtract_reduce_fusion.5 = (f32[8192]{0:T(1024)S(1)}, f32[140,8192]{1,0:T(8,128)}, f32[140,8192]{1,0:T(8,128)}) fusion(f32[140,8192]{1,0:T(8,128)} %get-tuple-element.497, f32[140,8192]{1,0:T(8,128)} %get-tuple-element.496, pred[]{:T(512)S(6)} %compare.3, f32[8192]{0:T(1024)S(1)} %get-tuple-element.516, f32[8192]{0:T(1024)S(1)} %bitcast.137, ...), kind=kOutput, calls=%fused_computation.21.clone.1 | convolution fusion | flops 314040320 | bytes 19567716 | tf_op jit(solution)/shard_map/while/body/eval_jaxpr/dot_general | solution.py:49
  416.8 8.4 %subtract_reduce_fusion.5 = (f32[8192]{0:T(1024)S(1)}, f32[140,8192]{1,0:T(8,128)}, f32[140,8192]{1,0:T(8,128)}) fusion(f32[140,8192]{1,0:T(8,128)} %get-tuple-element.497, f32[140,8192]{1,0:T(8,128)} %get-tuple-element.496, pred[]{:T(512)S(6)} %compare.3, f32[8192]{0:T(1024)S(1)} %get-tuple-element.516, f32[8192]{0:T(1024)S(1)} %bitcast.137, ...), kind=kOutput, calls=%fused_computation.21.clone.1 | convolution fusion | flops 314040320 | bytes 19567716 | tf_op jit(solution)/shard_map/while/body/eval_jaxpr/dot_general | solution.py:49
  426.6 8.4 %subtract_reduce_fusion.5 = (f32[8192]{0:T(1024)S(1)}, f32[140,8192]{1,0:T(8,128)}, f32[140,8192]{1,0:T(8,128)}) fusion(f32[140,8192]{1,0:T(8,128)} %get-tuple-element.497, f32[140,8192]{1,0:T(8,128)} %get-tuple-element.496, pred[]{:T(512)S(6)} %compare.3, f32[8192]{0:T(1024)S(1)} %get-tuple-element.516, f32[8192]{0:T(1024)S(1)} %bitcast.137, ...), kind=kOutput, calls=%fused_computation.21.clone.1 | convolution fusion | flops 314040320 | bytes 19567716 | tf_op jit(solution)/shard_map/while/body/eval_jaxpr/dot_general | solution.py:49
  436.5 8.4 %subtract_reduce_fusion.5 = (f32[8192]{0:T(1024)S(1)}, f32[140,8192]{1,0:T(8,128)}, f32[140,8192]{1,0:T(8,128)}) fusion(f32[140,8192]{1,0:T(8,128)} %get-tuple-element.497, f32[140,8192]{1,0:T(8,128)} %get-tuple-element.496, pred[]{:T(512)S(6)} %compare.3, f32[8192]{0:T(1024)S(1)} %get-tuple-element.516, f32[8192]{0:T(1024)S(1)} %bitcast.137, ...), kind=kOutput, calls=%fused_computation.21.clone.1 | convolution fusion | flops 314040320 | bytes 19567716 | tf_op jit(solution)/shard_map/while/body/eval_jaxpr/dot_general | solution.py:49
  446.3 8.4 %subtract_reduce_fusion.5 = (f32[8192]{0:T(1024)S(1)}, f32[140,8192]{1,0:T(8,128)}, f32[140,8192]{1,0:T(8,128)}) fusion(f32[140,8192]{1,0:T(8,128)} %get-tuple-element.497, f32[140,8192]{1,0:T(8,128)} %get-tuple-element.496, pred[]{:T(512)S(6)} %compare.3, f32[8192]{0:T(1024)S(1)} %get-tuple-element.516, f32[8192]{0:T(1024)S(1)} %bitcast.137, ...), kind=kOutput, calls=%fused_computation.21.clone.1 | convolution fusion | flops 314040320 | bytes 19567716 | tf_op jit(solution)/shard_map/while/body/eval_jaxpr/dot_general | solution.py:49
  456.2 8.4 %subtract_reduce_fusion.5 = (f32[8192]{0:T(1024)S(1)}, f32[140,8192]{1,0:T(8,128)}, f32[140,8192]{1,0:T(8,128)}) fusion(f32[140,8192]{1,0:T(8,128)} %get-tuple-element.497, f32[140,8192]{1,0:T(8,128)} %get-tuple-element.496, pred[]{:T(512)S(6)} %compare.3, f32[8192]{0:T(1024)S(1)} %get-tuple-element.516, f32[8192]{0:T(1024)S(1)} %bitcast.137, ...), kind=kOutput, calls=%fused_computation.21.clone.1 | convolution fusion | flops 314040320 | bytes 19567716 | tf_op jit(solution)/shard_map/while/body/eval_jaxpr/dot_general | solution.py:49
  466.1 8.4 %subtract_reduce_fusion.5 = (f32[8192]{0:T(1024)S(1)}, f32[140,8192]{1,0:T(8,128)}, f32[140,8192]{1,0:T(8,128)}) fusion(f32[140,8192]{1,0:T(8,128)} %get-tuple-element.497, f32[140,8192]{1,0:T(8,128)} %get-tuple-element.496, pred[]{:T(512)S(6)} %compare.3, f32[8192]{0:T(1024)S(1)} %get-tuple-element.516, f32[8192]{0:T(1024)S(1)} %bitcast.137, ...), kind=kOutput, calls=%fused_computation.21.clone.1 | convolution fusion | flops 314040320 | bytes 19567716 | tf_op jit(solution)/shard_map/while/body/eval_jaxpr/dot_general | solution.py:49
  475.9 8.4 %subtract_reduce_fusion.5 = (f32[8192]{0:T(1024)S(1)}, f32[140,8192]{1,0:T(8,128)}, f32[140,8192]{1,0:T(8,128)}) fusion(f32[140,8192]{1,0:T(8,128)} %get-tuple-element.497, f32[140,8192]{1,0:T(8,128)} %get-tuple-element.496, pred[]{:T(512)S(6)} %compare.3, f32[8192]{0:T(1024)S(1)} %get-tuple-element.516, f32[8192]{0:T(1024)S(1)} %bitcast.137, ...), kind=kOutput, calls=%fused_computation.21.clone.1 | convolution fusion | flops 314040320 | bytes 19567716 | tf_op jit(solution)/shard_map/while/body/eval_jaxpr/dot_general | solution.py:49
  485.8 8.4 %subtract_reduce_fusion.5 = (f32[8192]{0:T(1024)S(1)}, f32[140,8192]{1,0:T(8,128)}, f32[140,8192]{1,0:T(8,128)}) fusion(f32[140,8192]{1,0:T(8,128)} %get-tuple-element.497, f32[140,8192]{1,0:T(8,128)} %get-tuple-element.496, pred[]{:T(512)S(6)} %compare.3, f32[8192]{0:T(1024)S(1)} %get-tuple-element.516, f32[8192]{0:T(1024)S(1)} %bitcast.137, ...), kind=kOutput, calls=%fused_computation.21.clone.1 | convolution fusion | flops 314040320 | bytes 19567716 | tf_op jit(solution)/shard_map/while/body/eval_jaxpr/dot_general | solution.py:49
  495.7 8.4 %subtract_reduce_fusion.5 = (f32[8192]{0:T(1024)S(1)}, f32[140,8192]{1,0:T(8,128)}, f32[140,8192]{1,0:T(8,128)}) fusion(f32[140,8192]{1,0:T(8,128)} %get-tuple-element.497, f32[140,8192]{1,0:T(8,128)} %get-tuple-element.496, pred[]{:T(512)S(6)} %compare.3, f32[8192]{0:T(1024)S(1)} %get-tuple-element.516, f32[8192]{0:T(1024)S(1)} %bitcast.137, ...), kind=kOutput, calls=%fused_computation.21.clone.1 | convolution fusion | flops 314040320 | bytes 19567716 | tf_op jit(solution)/shard_map/while/body/eval_jaxpr/dot_general | solution.py:49
  505.5 8.4 %subtract_reduce_fusion.5 = (f32[8192]{0:T(1024)S(1)}, f32[140,8192]{1,0:T(8,128)}, f32[140,8192]{1,0:T(8,128)}) fusion(f32[140,8192]{1,0:T(8,128)} %get-tuple-element.497, f32[140,8192]{1,0:T(8,128)} %get-tuple-element.496, pred[]{:T(512)S(6)} %compare.3, f32[8192]{0:T(1024)S(1)} %get-tuple-element.516, f32[8192]{0:T(1024)S(1)} %bitcast.137, ...), kind=kOutput, calls=%fused_computation.21.clone.1 | convolution fusion | flops 314040320 | bytes 19567716 | tf_op jit(solution)/shard_map/while/body/eval_jaxpr/dot_general | solution.py:49
  515.4 8.4 %subtract_reduce_fusion.5 = (f32[8192]{0:T(1024)S(1)}, f32[140,8192]{1,0:T(8,128)}, f32[140,8192]{1,0:T(8,128)}) fusion(f32[140,8192]{1,0:T(8,128)} %get-tuple-element.497, f32[140,8192]{1,0:T(8,128)} %get-tuple-element.496, pred[]{:T(512)S(6)} %compare.3, f32[8192]{0:T(1024)S(1)} %get-tuple-element.516, f32[8192]{0:T(1024)S(1)} %bitcast.137, ...), kind=kOutput, calls=%fused_computation.21.clone.1 | convolution fusion | flops 314040320 | bytes 19567716 | tf_op jit(solution)/shard_map/while/body/eval_jaxpr/dot_general | solution.py:49
  525.2 8.4 %subtract_reduce_fusion.5 = (f32[8192]{0:T(1024)S(1)}, f32[140,8192]{1,0:T(8,128)}, f32[140,8192]{1,0:T(8,128)}) fusion(f32[140,8192]{1,0:T(8,128)} %get-tuple-element.497, f32[140,8192]{1,0:T(8,128)} %get-tuple-element.496, pred[]{:T(512)S(6)} %compare.3, f32[8192]{0:T(1024)S(1)} %get-tuple-element.516, f32[8192]{0:T(1024)S(1)} %bitcast.137, ...), kind=kOutput, calls=%fused_computation.21.clone.1 | convolution fusion | flops 314040320 | bytes 19567716 | tf_op jit(solution)/shard_map/while/body/eval_jaxpr/dot_general | solution.py:49
  535.1 8.4 %subtract_reduce_fusion.5 = (f32[8192]{0:T(1024)S(1)}, f32[140,8192]{1,0:T(8,128)}, f32[140,8192]{1,0:T(8,128)}) fusion(f32[140,8192]{1,0:T(8,128)} %get-tuple-element.497, f32[140,8192]{1,0:T(8,128)} %get-tuple-element.496, pred[]{:T(512)S(6)} %compare.3, f32[8192]{0:T(1024)S(1)} %get-tuple-element.516, f32[8192]{0:T(1024)S(1)} %bitcast.137, ...), kind=kOutput, calls=%fused_computation.21.clone.1 | convolution fusion | flops 314040320 | bytes 19567716 | tf_op jit(solution)/shard_map/while/body/eval_jaxpr/dot_general | solution.py:49
  545.0 8.4 %subtract_reduce_fusion.5 = (f32[8192]{0:T(1024)S(1)}, f32[140,8192]{1,0:T(8,128)}, f32[140,8192]{1,0:T(8,128)}) fusion(f32[140,8192]{1,0:T(8,128)} %get-tuple-element.497, f32[140,8192]{1,0:T(8,128)} %get-tuple-element.496, pred[]{:T(512)S(6)} %compare.3, f32[8192]{0:T(1024)S(1)} %get-tuple-element.516, f32[8192]{0:T(1024)S(1)} %bitcast.137, ...), kind=kOutput, calls=%fused_computation.21.clone.1 | convolution fusion | flops 314040320 | bytes 19567716 | tf_op jit(solution)/shard_map/while/body/eval_jaxpr/dot_general | solution.py:49
  554.8 8.4 %subtract_reduce_fusion.5 = (f32[8192]{0:T(1024)S(1)}, f32[140,8192]{1,0:T(8,128)}, f32[140,8192]{1,0:T(8,128)}) fusion(f32[140,8192]{1,0:T(8,128)} %get-tuple-element.497, f32[140,8192]{1,0:T(8,128)} %get-tuple-element.496, pred[]{:T(512)S(6)} %compare.3, f32[8192]{0:T(1024)S(1)} %get-tuple-element.516, f32[8192]{0:T(1024)S(1)} %bitcast.137, ...), kind=kOutput, calls=%fused_computation.21.clone.1 | convolution fusion | flops 314040320 | bytes 19567716 | tf_op jit(solution)/shard_map/while/body/eval_jaxpr/dot_general | solution.py:49
  564.7 8.4 %subtract_reduce_fusion.5 = (f32[8192]{0:T(1024)S(1)}, f32[140,8192]{1,0:T(8,128)}, f32[140,8192]{1,0:T(8,128)}) fusion(f32[140,8192]{1,0:T(8,128)} %get-tuple-element.497, f32[140,8192]{1,0:T(8,128)} %get-tuple-element.496, pred[]{:T(512)S(6)} %compare.3, f32[8192]{0:T(1024)S(1)} %get-tuple-element.516, f32[8192]{0:T(1024)S(1)} %bitcast.137, ...), kind=kOutput, calls=%fused_computation.21.clone.1 | convolution fusion | flops 314040320 | bytes 19567716 | tf_op jit(solution)/shard_map/while/body/eval_jaxpr/dot_general | solution.py:49
  574.6 8.4 %subtract_reduce_fusion.5 = (f32[8192]{0:T(1024)S(1)}, f32[140,8192]{1,0:T(8,128)}, f32[140,8192]{1,0:T(8,128)}) fusion(f32[140,8192]{1,0:T(8,128)} %get-tuple-element.497, f32[140,8192]{1,0:T(8,128)} %get-tuple-element.496, pred[]{:T(512)S(6)} %compare.3, f32[8192]{0:T(1024)S(1)} %get-tuple-element.516, f32[8192]{0:T(1024)S(1)} %bitcast.137, ...), kind=kOutput, calls=%fused_computation.21.clone.1 | convolution fusion | flops 314040320 | bytes 19567716 | tf_op jit(solution)/shard_map/while/body/eval_jaxpr/dot_general | solution.py:49
  594.8 7.2 %all-to-all-done = f32[8,8,30,128]{3,1,2,0:T(8,128)S(1)} async-done(((f32[8,8,30,128]{3,1,2,0:T(8,128)}), f32[8,8,30,128]{3,1,2,0:T(8,128)S(1)}, u32[]{:S(2)}, u32[]{:S(2)}) %all-to-all-start) | async-done | bytes 983072 | tf_op jit(solution)/shard_map/all_to_all | solution.py:192
  (332 shorter events, 245.6 us)
Async XLA Ops:
  7.2 3.5 copy-start.1
  7.2 3.5 copy-start.2
  7.2 48.6 %all-gather.3.cloned.1.call-start = ((), (), s32[]{:S(2)}) async-start(), calls=%async_computation.1 | async-start | bytes 6635520 | tf_op jit(solution)/shard_map/all_gather | solution.py:172
  9.6 9.9 %copy-start.6 = (s32[1,32,1]{1,2,0:T(1,128)S(1)}, s32[1,32,1]{1,2,0:T(1,128)}, u32[]{:S(2)}) copy-start(s32[1,32,1]{1,2,0:T(1,128)} %param.19) | copy-start | bytes 388
  9.7 17.7 %copy-start.8 = (s32[1,32]{1,0:T(1,128)S(1)}, s32[1,32]{1,0:T(1,128)}, u32[]{:S(2)}) copy-start(s32[1,32]{1,0:T(1,128)} %param.18) | copy-start | bytes 388
  9.7 17.7 %copy-start.3 = (f32[32,128]{1,0:T(8,128)S(1)}, f32[32,128]{1,0:T(8,128)}, u32[]{:S(2)}) copy-start(f32[32,128]{1,0:T(8,128)} %param.17) | copy-start | bytes 49156
  9.7 27.5 %copy-start.4 = (f32[140]{0:T(256)S(1)}, f32[140]{0:T(256)}, u32[]{:S(2)}) copy-start(f32[140]{0:T(256)} %param.23) | copy-start | bytes 1684
  12.3 28.6 %collective-permute-start = (f32[2,30,32,1]{2,0,3,1:T(2,128)S(1)}, f32[2,30,32,1]{2,0,3,1:T(2,128)S(1)}, u32[]{:S(2)}, u32[]{:S(2)}) collective-permute-start(f32[2,30,32,1]{2,0,3,1:T(2,128)S(1)} %copy.52), channel_id=1, source_target_pairs={{0,4},{4,8},{8,12},{12,16},{16,20},{20,24},{24,28},{1,5},{5,9},{9,... | collective-permute-start | bytes 23048 | tf_op jit(solution)/shard_map/ppermute | solution.py:19
  15.0 24.9 %collective-permute-start.1 = (f32[2,30,32,1]{2,0,3,1:T(2,128)S(1)}, f32[2,30,32,1]{2,0,3,1:T(2,128)S(1)}, u32[]{:S(2)}, u32[]{:S(2)}) collective-permute-start(f32[2,30,32,1]{2,0,3,1:T(2,128)S(1)} %copy.53), channel_id=1, source_target_pairs={{4,0},{8,4},{12,8},{16,12},{20,16},{24,20},{28,24},{5,1},{9,5},{13... | collective-permute-start | bytes 23048 | tf_op jit(solution)/shard_map/ppermute | solution.py:22
  42.1 6.2 %collective-permute-start.2 = (f32[2,30,1,130]{3,1,2,0:T(8,128)S(1)}, f32[2,30,1,130]{3,1,2,0:T(8,128)S(1)}, u32[]{:S(2)}, u32[]{:S(2)}) collective-permute-start(f32[2,30,1,130]{3,1,2,0:T(8,128)S(1)} %get-tuple-element.348), channel_id=1, source_target_pairs={{1,0},{2,1},{3,2},{5,4},{6,5},{7,6},{9,8},{10,9},{11,10},{13,12},{... | collective-permute-start | bytes 93608 | tf_op jit(solution)/shard_map/ppermute | solution.py:22
  44.4 6.2 %collective-permute-start.3 = (f32[2,30,1,130]{3,1,2,0:T(8,128)S(1)}, f32[2,30,1,130]{3,1,2,0:T(8,128)S(1)}, u32[]{:S(2)}, u32[]{:S(2)}) collective-permute-start(f32[2,30,1,130]{3,1,2,0:T(8,128)S(1)} %get-tuple-element.349), channel_id=1, source_target_pairs={{0,1},{1,2},{2,3},{4,5},{5,6},{6,7},{8,9},{9,10},{10,11},{12,13},{... | collective-permute-start | bytes 93608 | tf_op jit(solution)/shard_map/ppermute | solution.py:19
  63.6 4.1 copy-start.5
  63.7 6.8 %copy-start.7 = (f32[140]{0:T(256)S(1)}, f32[140]{0:T(256)}, u32[]{:S(2)}) copy-start(f32[140]{0:T(256)} %param.21) | copy-start | bytes 1684
  583.2 5.6 copy-start
  584.5 17.5 %all-to-all-start = ((f32[8,8,30,128]{3,1,2,0:T(8,128)}), f32[8,8,30,128]{3,1,2,0:T(8,128)S(1)}, u32[]{:S(2)}, u32[]{:S(2)}) async-start(f32[8,8,30,128]{3,1,2,0:T(8,128)} %copy.61), calls=%async_computation | async-start | bytes 1966080 | tf_op jit(solution)/shard_map/all_to_all | solution.py:192
Sparse Core Ops, SparseCore 0:
  10.8 44.9 all-gather.2
where the time goes:
time: 615 us; the launch traced here: 611 us
  matrix products  426 us (69%)
  other arithmetic  97.2 us (16%)
  local copies, waits for them, and re-layouts  25.1 us (4%)
  blocking collectives  17 us (3%)
  starting transfers between devices  16.8 us (3%)
  between operations  14.4 us (2%)
  waiting for transfers between devices  12.5 us (2%)
    dot_general x60, matrix products, optical_depth(): jnp.dot(table_layer, weights, preferred_element_type=jnp.float32)  422 us
    min x30, other arithmetic, optical_depth(): temp_pos = jnp.clip((air_temp + 3.0) * ((NT - 1.0) / 6.0), 0.0, NT - 1.0)  36.1 us
    add x30, other arithmetic, downward(): source = planck_emission_factor[:, None] * (1.0 + 0.25 * layer[0][None, :])  36 us
  transfers between devices with their start and end apart: 6, of which 4 were waited for; matrix products, arithmetic and copies ran while one was open for 3% of the time, Pallas kernels for 0%

commit v1 on v0

v1 whole, which is shorter than its diff:
```python
import functools
import math

import jax
import jax.numpy as jnp
from jax import lax
from jax.experimental import pallas as pl
from jax.experimental.pallas import tpu as pltpu
from jax.sharding import PartitionSpec as P

NT = 16
NQ = 8
NODES = NT * NQ
LANES = 128
ROWS = 8

diffusion = 0.2
diffusivity = 1.66
LOG2E = math.log2(math.e)

BF = jnp.bfloat16
F32 = jnp.float32


def rounded(x):
    return x.astype(BF).astype(F32)


def unrolled(count, most, body, carry):
    steps = max(n for n in range(1, most + 1) if count % n == 0)

    def several(o, carry):
        for k in range(steps):
            carry = body(o * steps + k, carry)
        return carry

    return lax.fori_loop(0, count // steps, several, carry)


def column_kernel(
    gpoints,
    t_ref,
    q_ref,
    c_ref,
    mu_ref,
    lit_ref,
    table_ref,
    cond_ref,
    planck_ref,
    insol_ref,
    total_ref,
    heat_ref,
    surface_ref,
    table_s,
    th_s,
    qh_s,
    dt_s,
    c_s,
    tr_s,
    beam_s,
    down_s,
    up_s,
):
    levels = t_ref.shape[0]
    padded = table_s.shape[1]
    tiles = padded // 16

    @pl.when(pl.program_id(0) == 0)
    def _():
        def prepare(l, _):
            layer = table_ref[l].astype(F32) * (-diffusivity * LOG2E)
            table_s[l] = jnp.concatenate(
                [layer, jnp.zeros((padded - gpoints, NODES), F32)], axis=0
            ).astype(BF)
            return 0

        lax.fori_loop(0, levels, prepare, 0)

    def hats(l, _):
        t = rounded(t_ref[l])
        q = rounded(q_ref[l])
        t_pos = jnp.clip((t + 3.0) * ((NT - 1.0) / 6.0), 0.0, NT - 1.0)
        q_pos = jnp.clip(q * (NQ - 1.0), 0.0, NQ - 1.0)
        for i in range(NT):
            th_s[l, i] = jnp.maximum(0.0, 1.0 - jnp.abs(t_pos - float(i)))
        for j in range(NQ):
            qh_s[l, j] = jnp.maximum(0.0, 1.0 - jnp.abs(q_pos - float(j)))
        following = rounded(t_ref[jnp.minimum(l + 1, levels - 1)])
        dt_s[l] = 0.25 * (t - following)
        c_s[l] = rounded(c_ref[l])
        return 0

    lax.fori_loop(0, levels, hats, 0)

    def spread(ref, index, row):
        return jnp.broadcast_to(ref[*index, pl.ds(row, 1), :], (ROWS, LANES))

    def wide(ref, index, row):
        one = spread(ref, index, row)
        return jnp.concatenate([one, one], axis=0).astype(BF)

    def weights(l, row):
        qh = jnp.concatenate(
            [qh_s[l, j, pl.ds(row, 1), :] for j in range(NQ)] * 2, axis=0
        ).astype(BF)
        parts = []
        for m in range(NT // 2):
            pair = jnp.concatenate(
                [spread(th_s, (l, 2 * m), row), spread(th_s, (l, 2 * m + 1), row)], axis=0
            ).astype(BF)
            parts.append(pair * qh)
        cloud = wide(c_s, (l,), row)
        return jnp.concatenate(parts + [cloud] * (NODES // 16), axis=0)

    def both(make):
        return jnp.concatenate([make(0), make(1)], axis=1)

    def per_point(ref, k):
        tile = ref[16 * k : 16 * k + 16, :]
        return jnp.concatenate([tile, tile], axis=1)

    def put(ref, l, first, parts):
        pairs = [parts[k] + parts[k + 1] for k in range(0, tiles - 1, 2)]
        if tiles % 2:
            pairs.append(parts[-1])
        total = sum(pair.astype(F32) for pair in pairs)
        total = total[:ROWS] + total[ROWS:]
        for h in range(2):
            at = pl.ds(pl.multiple_of((first + h) * ROWS, ROWS), ROWS)
            ref[l, at, :] = total[:, h * LANES : (h + 1) * LANES]

    def pair_of_rows(p, _):
        first = 2 * p

        def inverse_of(h):
            one = (1.0 / diffusivity) / rounded(mu_ref[pl.ds(first + h, 1), :])
            return jnp.broadcast_to(one, (16, LANES)).astype(BF)

        inverse = both(inverse_of)
        lit = both(lambda h: wide(lit_ref, (), first + h))
        start = both(lambda h: wide(t_ref, (0,), first + h)) * jnp.asarray(-0.25, BF) - jnp.asarray(
            1.0, BF
        )

        def transmit(l, _):
            rhs = both(lambda h: weights(l, first + h))
            lhs = jnp.concatenate([table_s[l], cond_ref[...]], axis=1)
            depth = jnp.dot(lhs, rhs, preferred_element_type=F32)
            for k in range(tiles):
                at = slice(16 * k, 16 * k + 16)
                part = depth[at].astype(BF)
                tr_s[l, at] = jnp.exp2(part)
                beam_s[l, at] = jnp.exp2(part * inverse)
            return 0

        def downward(l, carry):
            long, short = list(carry[0]), list(carry[1])
            step = both(lambda h: wide(dt_s, (l,), first + h))
            parts = []
            for k in range(tiles):
                at = slice(16 * k, 16 * k + 16)
                kept = tr_s[l, at] * long[k]
                short[k] = short[k] * beam_s[l, at]
                parts.append(kept + short[k])
                long[k] = kept + per_point(planck_ref, k) * step
            put(down_s, l, first, parts)
            return tuple(long), tuple(short)

        def upward(n, long):
            l = levels - 1 - n
            step = both(lambda h: wide(dt_s, (jnp.maximum(l - 1, 0),), first + h))
            long = list(long)
            parts = []
            for k in range(tiles):
                kept = tr_s[l, slice(16 * k, 16 * k + 16)] * long[k]
                parts.append(kept)
                long[k] = kept + per_point(planck_ref, k) * step
            put(up_s, l, first, parts)
            return tuple(long)

        unrolled(levels, 6, transmit, 0)
        unrolled(
            levels,
            6,
            downward,
            (
                tuple(per_point(planck_ref, k) * start for k in range(tiles)),
                tuple(per_point(insol_ref, k) * lit for k in range(tiles)),
            ),
        )
        zero = jnp.zeros((16, 2 * LANES), BF)
        unrolled(levels, 6, upward, (zero,) * tiles)
        return 0

    lax.fori_loop(0, ROWS // 2, pair_of_rows, 0)

    planck_total = total_ref[0, 0]
    insol_total = total_ref[0, 1]

    def gathered(ref, l):
        return sum(ref[l, pl.ds(k, ROWS, stride=ROWS), :] for k in range(ROWS))

    def finish(l, down_in):
        source = (1.0 + 0.25 * rounded(t_ref[l])) * planck_total
        after = jnp.minimum(l + 1, levels - 1)
        source_after = (1.0 + 0.25 * rounded(t_ref[after])) * planck_total
        down_out = gathered(down_s, l) + source
        up_out = source - gathered(up_s, l)
        up_in = jnp.where(l == levels - 1, source, source_after - gathered(up_s, after))
        heat_ref[l] = (2.0 / gpoints) * (down_in - down_out + up_in - up_out)
        return down_out

    bottom = lax.fori_loop(0, levels, finish, rounded(lit_ref[...]) * insol_total)
    surface_ref[...] = bottom * (1.0 / gpoints)


def halves(x):
    high = x.astype(BF)
    return high, (x - high.astype(F32)).astype(BF)


def whole(x):
    return pl.BlockSpec(x.shape, lambda i: (0,) * x.ndim)


def radiate(t, q, c, mu, lit, table, cond, planck, insol):
    levels, rows, width = t.shape
    gpoints = table.shape[1]
    padded = -(-gpoints // 16) * 16

    def spread(x):
        return jnp.broadcast_to(jnp.pad(x.astype(BF), (0, padded - gpoints))[:, None], (padded, LANES))

    cond_high, cond_low = halves(cond * (-diffusivity * LOG2E))
    cond_tile = jnp.pad(
        jnp.stack([cond_high, cond_low], axis=1), ((0, padded - gpoints), (0, NODES - 2))
    )
    total = jnp.stack([jnp.sum(rounded(planck)), jnp.sum(rounded(insol))])[None]
    grid3 = pl.BlockSpec((levels, ROWS, width), lambda i: (0, i, 0))
    grid2 = pl.BlockSpec((ROWS, width), lambda i: (i, 0))

    tall_planck, tall_insol = spread(planck), spread(insol)
    return pl.pallas_call(
        functools.partial(column_kernel, gpoints),
        grid=(rows // ROWS,),
        in_specs=[
            grid3,
            grid3,
            grid3,
            grid2,
            grid2,
            whole(table),
            whole(cond_tile),
            whole(tall_planck),
            whole(tall_insol),
            pl.BlockSpec(memory_space=pltpu.SMEM),
        ],
        out_specs=[grid3, grid2],
        out_shape=[
            jax.ShapeDtypeStruct((levels, rows, width), F32),
            jax.ShapeDtypeStruct((rows, width), F32),
        ],
        scratch_shapes=[
            pltpu.VMEM((levels, padded, NODES), BF),
            pltpu.VMEM((levels, NT, ROWS, LANES), F32),
            pltpu.VMEM((levels, NQ, ROWS, LANES), F32),
            pltpu.VMEM((levels, ROWS, LANES), F32),
            pltpu.VMEM((levels, ROWS, LANES), F32),
            pltpu.VMEM((levels, padded, 2 * LANES), BF),
            pltpu.VMEM((levels, padded, 2 * LANES), BF),
            pltpu.VMEM((levels, ROWS * ROWS, LANES), F32),
            pltpu.VMEM((levels, ROWS * ROWS, LANES), F32),
        ],
        compiler_params=pltpu.CompilerParams(vmem_limit_bytes=40 * 1024 * 1024),
        cost_estimate=pl.CostEstimate(
            flops=2 * levels * padded * 256 * rows * width,
            bytes_accessed=4 * 4 * levels * rows * width,
            transcendentals=2 * levels * padded * rows * width,
        ),
        name="columns",
    )(t, q, c, mu, lit, table, cond_tile, tall_planck, tall_insol, total)


def edge_kernel(t_ref, q_ref, sides_ref, low_ref, high_ref):
    levels, rows, width = t_ref.shape
    lane = lax.broadcasted_iota(jnp.int32, (rows, width), 1)

    def body(l, packed):
        for k, ref in enumerate((t_ref, q_ref)):
            n = k * levels + l
            v = ref[l]
            low_ref[pl.ds(n, 1), :] = v[:1]
            high_ref[pl.ds(n, 1), :] = v[rows - 1 :]
            packed = jnp.where(lane // 2 == n, pltpu.roll(v, 2 * n + 1, axis=1), packed)
        return packed

    sides_ref[...] = unrolled(levels, 6, body, jnp.zeros((rows, width), F32))


def edges(t, q):
    levels, rows, width = t.shape
    line = jax.ShapeDtypeStruct((2 * levels, width), F32)
    return pl.pallas_call(
        edge_kernel,
        out_shape=[jax.ShapeDtypeStruct((rows, width), F32), line, line],
        name="edges",
    )(t, q)


def stencil_kernel(
    levels, t_ref, q_ref, heat_ref, west_ref, east_ref, south_ref, north_ref, t_out, q_out
):
    count, rows, width = t_ref.shape
    lane = lax.broadcasted_iota(jnp.int32, (rows, width), 1)
    row = lax.broadcasted_iota(jnp.int32, (rows, width), 0)
    sides = jnp.where(
        lane % 2 == 0,
        pltpu.roll(east_ref[...], width - 1, axis=1),
        pltpu.roll(west_ref[...], 1, axis=1),
    )

    def smoothed(v, n):
        halo = pltpu.roll(sides, width - 1 - 2 * n, axis=1)
        west = jnp.where(lane == 0, halo, pltpu.roll(v, 1, axis=1))
        east = jnp.where(lane == width - 1, halo, pltpu.roll(v, width - 1, axis=1))
        south = jnp.where(row == 0, south_ref[pl.ds(n, 1), :], pltpu.roll(v, 1, axis=0))
        north = jnp.where(row == rows - 1, north_ref[pl.ds(n, 1), :], pltpu.roll(v, rows - 1, axis=0))
        return v + diffusion * (((north + south) + (east + west)) - 4.0 * v)

    for j in range(count):
        l = pl.program_id(0) * count + j
        t_out[j] = smoothed(t_ref[j], l) + heat_ref[j]
        q_out[j] = smoothed(q_ref[j], levels + l)


def diffuse(t, q, heating, west, east, south, north):
    levels, rows, width = t.shape
    count = max(n for n in range(1, 7) if levels % n == 0)
    block = pl.BlockSpec((count, rows, width), lambda i: (i, 0, 0))
    out = jax.ShapeDtypeStruct(t.shape, F32)
    return pl.pallas_call(
        functools.partial(stencil_kernel, levels),
        grid=(levels // count,),
        in_specs=[block, block, block, whole(west), whole(east), whole(south), whole(north)],
        out_specs=[block, block],
        out_shape=[out, out],
        name="diffuse",
    )(t, q, heating, west, east, south, north)


def neighbours(low_edge, high_edge, axis):
    count = lax.axis_size(axis)
    forward = [(i, i + 1) for i in range(count - 1)]
    backward = [(target, source) for source, target in forward]
    return lax.ppermute(high_edge, axis, forward), lax.ppermute(low_edge, axis, backward)


def block_rank(hosts):
    count = hosts.shape[-1]
    earlier = jnp.arange(count)[None, :] < jnp.arange(count)[:, None]
    same = hosts[:, None] == hosts[None, :]
    return jnp.sum(jnp.logical_and(same, earlier), axis=-1)


def on_device(
    thermal_anomaly_grid,
    relative_moisture,
    overcast_share,
    sun_angle_projection,
    daylight_mask,
    radiator_owner_position,
    molecular_opacity_lookup,
    condensed_opacity_per_share,
    planck_emission_factor,
    insolation_quadrature_factor,
):
    host_count = lax.axis_size("gx")
    t, q = thermal_anomaly_grid, relative_moisture
    blocks = t.shape[1]
    capacity = max(2, (2 * blocks + host_count - 1) // host_count)

    sides, low, high = edges(t, q)
    west, east = neighbours(sides, sides, "gx")
    south, north = neighbours(low, high, "gy")

    lit = sun_angle_projection * daylight_mask[0].astype(F32)[:, None]
    heating, surface = radiate(
        t,
        q,
        overcast_share,
        sun_angle_projection,
        lit,
        molecular_opacity_lookup,
        condensed_opacity_per_share,
        planck_emission_factor,
        insolation_quadrature_factor,
    )

    hosts = radiator_owner_position[0, :, 0]
    slot = hosts * capacity + block_rank(hosts)
    chosen = (jnp.arange(host_count * capacity)[:, None] == slot[None, :]).astype(F32)
    sent = jnp.dot(chosen, surface, precision=lax.Precision.HIGHEST)
    slots = lax.all_to_all(
        sent.reshape(host_count, capacity, surface.shape[1]),
        "gx",
        split_axis=0,
        concat_axis=0,
        tiled=True,
    )

    t_next, q_next = diffuse(t, q, heating, west, east, south, north)
    return t_next, q_next, slots[None, None]


def solution(mesh):
    placed = (
        P(None, "gy", "gx"),
        P(None, "gy", "gx"),
        P(None, "gy", "gx"),
        P("gy", "gx"),
        P("gx", "gy"),
        P("gx", "gy", None),
        P(),
        P(),
        P(),
        P(),
    )
    return jax.shard_map(
        on_device,
        mesh=mesh,
        in_specs=placed,
        out_specs=(P(None, "gy", "gx"), P(None, "gy", "gx"), P("gy", "gx", None, None, None)),
        check_vma=False,
    )
```

time: 615 us -> 101 us (0.16)
  the two profiles are of different devices: /device:TPU:20 before, /device:TPU:27 now
where the time goes in v1:
time: 101 us; the launch traced here: 100 us
  Pallas kernels  69.5 us (69%)
  starting transfers between devices  15.7 us (16%)
  other arithmetic  4.92 us (5%)
  local copies, waits for them, and re-layouts  4.62 us (5%)
  waiting for transfers between devices  4.01 us (4%)
    pallas_call x1, Pallas kernels, radiate(): pl.pallas_call(functools.partial(column_kernel, gpoints), grid=(rows // R...  62.5 us
    ppermute x2, starting transfers between devices, neighbours(): lax.ppermute(low_edge, axis, backward)  5.91 us
    all_to_all x1, starting transfers between devices, on_device(): lax.all_to_all(sent.reshape(host_count, capacity, surface.shape[1]), 'gx'...  5.14 us
    ppermute x2, starting transfers between devices, neighbours(): lax.ppermute(high_edge, axis, forward)  4.61 us
    pallas_call x1, Pallas kernels, diffuse(): pl.pallas_call(functools.partial(stencil_kernel, levels), grid=(levels //...  4.55 us
    unnamed x27, local copies, waits for them, and re-layouts  4.29 us
    ppermute x2, waiting for transfers between devices, neighbours(): lax.ppermute(low_edge, axis, backward)  4 us
    reduce_sum x2, other arithmetic, radiate(): total = jnp.stack([jnp.sum(rounded(planck)), jnp.sum(rounded(insol))])[None]  2.6 us
  transfers between devices with their start and end apart: 5, of which 1 were waited for; matrix products, arithmetic and copies ran while one was open for 6% of the time, Pallas kernels for 62%

profile of v1, /device:TPU:27, one launch (start us, length us, event | category | flops | bytes accessed | tf_op | source)
XLA Modules:
  0.0 100.3 jit_solution(12327994333700111263)
XLA Ops:
  0.6 0.0 copy-start
  0.6 0.0 copy-start.1
  0.7 0.0 copy-start.11
  0.7 0.0 copy-start.12
  0.7 0.0 copy-start.3
  0.7 2.4 %edges.1 = (f32[32,128]{1,0:T(8,128)}, f32[60,128]{1,0:T(8,128)}, f32[60,128]{1,0:T(8,128)}) custom-call(f32[30,32,128]{2,1,0:T(8,128)} %t_ref.5, f32[30,32,128]{2,1,0:T(8,128)} %q_ref.5), custom_call_target="tpu_custom_call" | custom-call | tf_op jit(solution)/shard_map/edges/pallas_call | solution.py:303
  3.1 1.3 %collective-permute-start.2 = (f32[60,128]{1,0:T(8,128)}, f32[60,128]{1,0:T(8,128)S(1)}, u32[]{:S(2)}, u32[]{:S(2)}) collective-permute-start(f32[60,128]{1,0:T(8,128)} %get-tuple-element.12), channel_id=1, source_target_pairs={{0,1},{1,2},{2,3},{4,5},{5,6},{6,7},{8,9},{9,10},{10,11},{12,13},{... | collective-permute-start | bytes 92168 | tf_op jit(solution)/shard_map/ppermute | solution.py:355
  4.4 4.0 %collective-permute-start.3 = (f32[60,128]{1,0:T(8,128)}, f32[60,128]{1,0:T(8,128)S(1)}, u32[]{:S(2)}, u32[]{:S(2)}) collective-permute-start(f32[60,128]{1,0:T(8,128)} %get-tuple-element.13), channel_id=1, source_target_pairs={{1,0},{2,1},{3,2},{5,4},{6,5},{7,6},{9,8},{10,9},{11,10},{13,12},{... | collective-permute-start | bytes 92168 | tf_op jit(solution)/shard_map/ppermute | solution.py:355
  8.4 0.7 multiply_convert_fusion
  9.1 0.1 copy.16
  9.3 1.3 %convert_reduce_fusion.2 = (f32[]{:T(128)}, bf16[140]{0:T(256)(128)(2,1)S(1)}) fusion(f32[140]{0:T(256)} %param.18), kind=kLoop, calls=%fused_computation.9 | loop fusion | flops 419 | bytes 844 | tf_op jit(solution)/shard_map/reduce_sum | solution.py:238
  10.6 1.3 %convert_reduce_fusion.1 = (f32[]{:T(128)}, bf16[140]{0:T(256)(128)(2,1)S(1)}) fusion(f32[140]{0:T(256)} %param.19), kind=kLoop, calls=%fused_computation.8 | loop fusion | flops 419 | bytes 844 | tf_op jit(solution)/shard_map/reduce_sum | solution.py:238
  11.9 0.0 copy-done.11
  11.9 0.0 copy-done.12
  11.9 0.2 convert_reduce_fusion
  12.1 1.4 %maximum_bitcast_fusion.total_ref = f32[1,2]{1,0:T(1,128)S(1)} fusion(f32[1]{0:T(128)} %bitcast.2, f32[1]{0:T(128)} %bitcast.1), kind=kLoop, calls=%fused_computation.12 | loop fusion | flops 2 | bytes 16 | tf_op jit(solution)/shard_map/broadcast_in_dim | solution.py:238
  13.5 0.0 copy-done.3
  13.5 0.1 broadcast_multiply_fusion.lit_ref
  13.6 0.1 broadcast_in_dim.8.planck_ref
  13.7 0.1 broadcast_in_dim.9.insol_ref
  13.7 0.0 copy-done
  13.8 0.0 copy-done.1
  13.8 0.0 copy-start.4
  13.8 1.2 %copy-done.4 = bf16[30,140,128]{2,1,0:T(8,128)(2,1)S(1)} copy-done((bf16[30,140,128]{2,1,0:T(8,128)(2,1)S(1)}, bf16[30,140,128]{2,1,0:T(8,128)(2,1)}, u32[]{:S(2)}) %copy-start.4) | copy-done | bytes 1075224
  15.0 0.0 copy-start.5
  15.0 1.0 %copy-done.5 = f32[30,32,128]{2,1,0:T(8,128)S(1)} copy-done((f32[30,32,128]{2,1,0:T(8,128)S(1)}, f32[30,32,128]{2,1,0:T(8,128)}, u32[]{:S(2)}) %copy-start.5) | copy-done | bytes 491544
  16.0 0.0 copy-start.10
  16.0 62.5 %columns.1 = (f32[30,32,128]{2,1,0:T(8,128)S(1)}, f32[32,128]{1,0:T(8,128)S(1)}) custom-call(f32[30,32,128]{2,1,0:T(8,128)S(1)} %copy-done, f32[30,32,128]{2,1,0:T(8,128)S(1)} %copy-done.1, f32[30,32,128]{2,1,0:T(8,128)S(1)} %copy-done.5, f32[32,128]{1,0:T(8,128)S(1)} %copy-done.3, f32[32,128]{1,0:T(8,128)S(1)} %broadcast_multiply_fusion.lit_ref, ...), custom_call_target="tpu_custom_call" | custom-call | flops 9059696640 | bytes 1966080 | tf_op jit(solution)/shard_map/columns/pallas_call | solution.py:243
  78.5 0.0 copy-start.2
  78.5 0.8 copy-done.2
  79.3 0.8 convolution_bitcast_fusion
  80.1 5.1 %all-to-all-start = ((f32[8,8,128]{2,1,0:T(8,128)}), f32[8,8,128]{2,1,0:T(8,128)S(1)}, u32[]{:S(2)}, u32[]{:S(2)}) async-start(f32[8,8,128]{2,1,0:T(8,128)} %convolution_bitcast_fusion), calls=%async_computation | async-start | bytes 65536 | tf_op jit(solution)/shard_map/all_to_all | solution.py:403
  85.2 0.0 copy-done.10
  85.2 3.3 %collective-permute-start = (f32[32,128]{1,0:T(8,128)S(1)}, f32[32,128]{1,0:T(8,128)S(1)}, u32[]{:S(2)}, u32[]{:S(2)}) collective-permute-start(f32[32,128]{1,0:T(8,128)S(1)} %copy-done.10), channel_id=1, source_target_pairs={{0,4},{4,8},{8,12},{12,16},{16,20},{20,24},{24,28},{1,5},{5,9},{9,... | collective-permute-start | bytes 49160 | tf_op jit(solution)/shard_map/ppermute | solution.py:355
  88.5 1.9 %collective-permute-start.1 = (f32[32,128]{1,0:T(8,128)S(1)}, f32[32,128]{1,0:T(8,128)S(1)}, u32[]{:S(2)}, u32[]{:S(2)}) collective-permute-start(f32[32,128]{1,0:T(8,128)S(1)} %copy-done.10), channel_id=1, source_target_pairs={{4,0},{8,4},{12,8},{16,12},{20,16},{24,20},{28,24},{5,1},{9,5},{13... | collective-permute-start | bytes 49160 | tf_op jit(solution)/shard_map/ppermute | solution.py:355
  90.5 0.0 all-to-all-done
  90.5 0.0 collective-permute-done.west_ref
  90.5 0.0 copy-start.8
  90.5 4.0 %collective-permute-done.1.east_ref = f32[32,128]{1,0:T(8,128)S(1)} collective-permute-done((f32[32,128]{1,0:T(8,128)S(1)}, f32[32,128]{1,0:T(8,128)S(1)}, u32[]{:S(2)}, u32[]{:S(2)}) %collective-permute-start.1) | collective-permute-done | bytes 16416 | tf_op jit(solution)/shard_map/ppermute | solution.py:355
  94.5 0.0 collective-permute-done.2.south_ref
  94.5 0.0 collective-permute-done.3.north_ref
  94.5 0.0 copy-start.7
  94.5 0.0 copy-done.8
  94.5 0.6 copy-done.9
  95.1 0.0 copy-done.6
  95.1 0.0 copy-done.7
  95.1 4.6 %diffuse.1 = (f32[30,32,128]{2,1,0:T(8,128)}, f32[30,32,128]{2,1,0:T(8,128)}) custom-call(f32[30,32,128]{2,1,0:T(8,128)} %t_ref.5, f32[30,32,128]{2,1,0:T(8,128)} %q_ref.5, f32[30,32,128]{2,1,0:T(8,128)} %copy-done.2, f32[32,128]{1,0:T(8,128)} %copy-done.8, f32[32,128]{1,0:T(8,128)} %copy-done.9, f32[60,128]{1,0:T(8,128)} %copy-done.6, f32[60,128]{1,0:T(8,128)} %copy-done.7), custom_call_target="tpu_custom_call" | custom-call | tf_op jit(solution)/shard_map/diffuse/pallas_call | solution.py:341
  99.7 0.6 copy.18
  (10 shorter events, 0.1 us)
Async XLA Ops:
  0.6 13.1 %copy-start = (f32[30,32,128]{2,1,0:T(8,128)S(1)}, f32[30,32,128]{2,1,0:T(8,128)}, u32[]{:S(2)}) copy-start(f32[30,32,128]{2,1,0:T(8,128)} %t_ref.5) | copy-start | bytes 1474564
  0.6 13.1 %copy-start.1 = (f32[30,32,128]{2,1,0:T(8,128)S(1)}, f32[30,32,128]{2,1,0:T(8,128)}, u32[]{:S(2)}) copy-start(f32[30,32,128]{2,1,0:T(8,128)} %q_ref.5) | copy-start | bytes 1474564
  0.7 11.3 %copy-start.11 = (s32[1,32]{1,0:T(1,128)S(1)}, s32[1,32]{1,0:T(1,128)}, u32[]{:S(2)}) copy-start(s32[1,32]{1,0:T(1,128)} %param.14) | copy-start | bytes 388
  0.7 11.3 %copy-start.12 = (s32[1,32,1]{1,2,0:T(1,128)S(1)}, s32[1,32,1]{1,2,0:T(1,128)}, u32[]{:S(2)}) copy-start(s32[1,32,1]{1,2,0:T(1,128)} %param.15) | copy-start | bytes 388
  0.7 12.8 %copy-start.3 = (f32[32,128]{1,0:T(8,128)S(1)}, f32[32,128]{1,0:T(8,128)}, u32[]{:S(2)}) copy-start(f32[32,128]{1,0:T(8,128)} %mu_ref.1) | copy-start | bytes 49156
  3.1 91.4 %collective-permute-start.2 = (f32[60,128]{1,0:T(8,128)}, f32[60,128]{1,0:T(8,128)S(1)}, u32[]{:S(2)}, u32[]{:S(2)}) collective-permute-start(f32[60,128]{1,0:T(8,128)} %get-tuple-element.12), channel_id=1, source_target_pairs={{0,1},{1,2},{2,3},{4,5},{5,6},{6,7},{8,9},{9,10},{10,11},{12,13},{... | collective-permute-start | bytes 92168 | tf_op jit(solution)/shard_map/ppermute | solution.py:355
  4.4 90.1 %collective-permute-start.3 = (f32[60,128]{1,0:T(8,128)}, f32[60,128]{1,0:T(8,128)S(1)}, u32[]{:S(2)}, u32[]{:S(2)}) collective-permute-start(f32[60,128]{1,0:T(8,128)} %get-tuple-element.13), channel_id=1, source_target_pairs={{1,0},{2,1},{3,2},{5,4},{6,5},{7,6},{9,8},{10,9},{11,10},{13,12},{... | collective-permute-start | bytes 92168 | tf_op jit(solution)/shard_map/ppermute | solution.py:355
  13.8 1.2 %copy-start.4 = (bf16[30,140,128]{2,1,0:T(8,128)(2,1)S(1)}, bf16[30,140,128]{2,1,0:T(8,128)(2,1)}, u32[]{:S(2)}) copy-start(bf16[30,140,128]{2,1,0:T(8,128)(2,1)} %table_ref.1) | copy-start | bytes 3225604
  15.0 1.0 %copy-start.5 = (f32[30,32,128]{2,1,0:T(8,128)S(1)}, f32[30,32,128]{2,1,0:T(8,128)}, u32[]{:S(2)}) copy-start(f32[30,32,128]{2,1,0:T(8,128)} %c_ref.1) | copy-start | bytes 1474564
  16.0 69.2 %copy-start.10 = (f32[32,128]{1,0:T(8,128)S(1)}, f32[32,128]{1,0:T(8,128)}, u32[]{:S(2)}) copy-start(f32[32,128]{1,0:T(8,128)} %get-tuple-element.11) | copy-start | bytes 49156
  78.5 0.8 copy-start.2
  80.1 10.4 %all-to-all-start = ((f32[8,8,128]{2,1,0:T(8,128)}), f32[8,8,128]{2,1,0:T(8,128)S(1)}, u32[]{:S(2)}, u32[]{:S(2)}) async-start(f32[8,8,128]{2,1,0:T(8,128)} %convolution_bitcast_fusion), calls=%async_computation | async-start | bytes 65536 | tf_op jit(solution)/shard_map/all_to_all | solution.py:403
  85.2 5.3 %collective-permute-start = (f32[32,128]{1,0:T(8,128)S(1)}, f32[32,128]{1,0:T(8,128)S(1)}, u32[]{:S(2)}, u32[]{:S(2)}) collective-permute-start(f32[32,128]{1,0:T(8,128)S(1)} %copy-done.10), channel_id=1, source_target_pairs={{0,4},{4,8},{8,12},{12,16},{16,20},{20,24},{24,28},{1,5},{5,9},{9,... | collective-permute-start | bytes 49160 | tf_op jit(solution)/shard_map/ppermute | solution.py:355
  88.5 6.0 %collective-permute-start.1 = (f32[32,128]{1,0:T(8,128)S(1)}, f32[32,128]{1,0:T(8,128)S(1)}, u32[]{:S(2)}, u32[]{:S(2)}) collective-permute-start(f32[32,128]{1,0:T(8,128)S(1)} %copy-done.10), channel_id=1, source_target_pairs={{4,0},{8,4},{12,8},{16,12},{20,16},{24,20},{28,24},{5,1},{9,5},{13... | collective-permute-start | bytes 49160 | tf_op jit(solution)/shard_map/ppermute | solution.py:355
  90.5 4.0 %copy-start.8 = (f32[32,128]{1,0:T(8,128)}, f32[32,128]{1,0:T(8,128)S(1)}, u32[]{:S(2)}) copy-start(f32[32,128]{1,0:T(8,128)S(1)} %collective-permute-done.west_ref) | copy-start | bytes 49156
  94.5 0.6 copy-start.9
  94.5 0.6 copy-start.6
  94.5 0.6 copy-start.7

commit v2 on v1

v2 whole, which is shorter than its diff:
```python
import functools
import math

import jax
import jax.numpy as jnp
from jax import lax
from jax.experimental import pallas as pl
from jax.experimental.pallas import tpu as pltpu
from jax.sharding import PartitionSpec as P

NT = 16
NQ = 8
NODES = NT * NQ
LANES = 128
ROWS = 8

diffusion = 0.2
diffusivity = 1.66
LOG2E = math.log2(math.e)

BF = jnp.bfloat16
F32 = jnp.float32


def rounded(x):
    return x.astype(BF).astype(F32)


def unrolled(count, most, body, carry):
    steps = max(n for n in range(1, most + 1) if count % n == 0)

    def several(o, carry):
        for k in range(steps):
            carry = body(o * steps + k, carry)
        return carry

    return lax.fori_loop(0, count // steps, several, carry)


def column_kernel(
    gpoints,
    capacity,
    hosts_ref,
    daylight_ref,
    t_ref,
    q_ref,
    c_ref,
    mu_ref,
    table_ref,
    planck_ref,
    insol_ref,
    cond_ref,
    heat_ref,
    slots_ref,
    table_s,
    cond_s,
    planck_s,
    insol_s,
    inverse_s,
    lit_s,
    points_s,
    th_s,
    qh_s,
    dt_s,
    tr_s,
    beam_s,
    down_s,
    up_s,
    surface_s,
    taken_s,
):
    levels, rows, _ = t_ref.shape
    padded = table_s.shape[1]
    tiles = padded // 16
    groups = rows // ROWS
    pairs = rows // 2

    def prepare(l, _):
        layer = table_ref[l].astype(F32) * (-diffusivity * LOG2E)
        table_s[l] = jnp.concatenate(
            [layer, jnp.zeros((padded - gpoints, NODES), F32)], axis=0
        ).astype(BF)
        return 0

    unrolled(levels, 3, prepare, 0)

    points_s[...] = jnp.zeros(points_s.shape, F32)
    for k, ref in enumerate((planck_ref, insol_ref, cond_ref)):
        points_s[k : k + 1, :gpoints] = ref[...]
    for r in range(rows):
        lit = mu_ref[r : r + 1, :] * daylight_ref[r].astype(F32)
        lit_s[r : r + 1, :] = rounded(lit)

    def column(k):
        line = jnp.broadcast_to(points_s[k : k + 1, :], (LANES, points_s.shape[1]))
        return jnp.transpose(line)[:padded]

    planck_s[...] = column(0).astype(BF)
    insol_s[...] = column(1).astype(BF)
    cond = column(2) * (-diffusivity * LOG2E)
    high = rounded(cond)
    lane = lax.broadcasted_iota(jnp.int32, (padded, LANES), 1)
    cond_s[...] = jnp.where(lane == 0, high, jnp.where(lane == 1, cond - high, 0.0)).astype(BF)
    inverse_s[...] = (1.0 / diffusivity) / rounded(mu_ref[...])

    def hats(l, _):
        after = jnp.minimum(l + 1, levels - 1)
        for g in range(groups):
            at = slice(g * ROWS, (g + 1) * ROWS)
            t = rounded(t_ref[l, at])
            t_pos = jnp.clip((t + 3.0) * ((NT - 1.0) / 6.0), 0.0, NT - 1.0)
            q_pos = jnp.clip(rounded(q_ref[l, at]) * (NQ - 1.0), 0.0, NQ - 1.0)
            for i in range(NT):
                th_s[g, l, i] = jnp.maximum(0.0, 1.0 - jnp.abs(t_pos - float(i)))
            for j in range(NQ):
                qh_s[g, l, j * ROWS : (j + 1) * ROWS] = jnp.maximum(
                    0.0, 1.0 - jnp.abs(q_pos - float(j))
                )
            dt_s[l, at] = 0.25 * (t - rounded(t_ref[after, at]))
        return 0

    unrolled(levels, 2, hats, 0)

    def spread(ref, index, row):
        return jnp.broadcast_to(ref[*index, pl.ds(row, 1), :], (ROWS, LANES))

    def wide(ref, index, row):
        one = spread(ref, index, row)
        return jnp.concatenate([one, one], axis=0).astype(BF)

    def weights(l, row):
        g, r = row // ROWS, row % ROWS
        qh = qh_s[g, l, pl.ds(r, NQ, stride=ROWS), :]
        qh = jnp.concatenate([qh, qh], axis=0).astype(BF)
        parts = []
        for m in range(NT // 2):
            pair = jnp.concatenate(
                [spread(th_s, (g, l, 2 * m), r), spread(th_s, (g, l, 2 * m + 1), r)], axis=0
            ).astype(BF)
            parts.append(pair * qh)
        cloud = wide(c_ref, (l,), row)
        return jnp.concatenate(parts + [cloud] * (NODES // 16), axis=0)

    def both(make):
        return jnp.concatenate([make(0), make(1)], axis=1)

    def tile(k):
        return slice(16 * k, 16 * k + 16)

    def put(ref, l, row, total):
        at = pl.ds(pl.multiple_of(row * ROWS, ROWS), ROWS)
        ref[l, at, :] = total[:ROWS] + total[ROWS:]

    def pair_of_rows(p, _):
        def transmit(l, _):
            rhs = both(lambda h: weights(l, 2 * p + h))
            lhs = jnp.concatenate([table_s[l], cond_s[...]], axis=1)
            depth = jnp.dot(lhs, rhs, preferred_element_type=F32)
            inverse = both(lambda h: wide(inverse_s, (), 2 * p + h))
            for k in range(tiles):
                part = depth[tile(k)].astype(BF)
                tr_s[l, tile(k)] = jnp.exp2(part)
                beam_s[l, tile(k)] = jnp.exp2(part * inverse)
            return 0

        unrolled(levels, 10, transmit, 0)

        for h in range(2):
            row = 2 * p + h
            lanes = slice(h * LANES, (h + 1) * LANES)

            def sweep(n, state):
                long, short, rising = (list(part) for part in state)
                m = levels - 1 - n
                step = wide(dt_s, (n,), row)
                up_step = wide(dt_s, (jnp.maximum(m - 1, 0),), row)
                down_total, up_total = 0.0, 0.0
                for k in range(0, tiles, 2):
                    down_part, up_part = 0.0, 0.0
                    for j in range(k, min(k + 2, tiles)):
                        planck = planck_s[tile(j)]
                        kept = tr_s[n, tile(j), lanes] * long[j]
                        short[j] = short[j] * beam_s[n, tile(j), lanes]
                        long[j] = kept + planck * step
                        risen = tr_s[m, tile(j), lanes] * rising[j]
                        rising[j] = risen + planck * up_step
                        down_part = kept + short[j] + down_part
                        up_part = risen + up_part
                    down_total = down_part.astype(F32) + down_total
                    up_total = up_part.astype(F32) + up_total
                put(down_s, n, row, down_total)
                put(up_s, m, row, up_total)
                return tuple(long), tuple(short), tuple(rising)

            start = wide(t_ref, (0,), row) * jnp.asarray(-0.25, BF) - jnp.asarray(1.0, BF)
            lit = wide(lit_s, (), row)
            state = (
                tuple(planck_s[tile(k)] * start for k in range(tiles)),
                tuple(insol_s[tile(k)] * lit for k in range(tiles)),
                (jnp.zeros((16, LANES), BF),) * tiles,
            )
            unrolled(levels, 6, sweep, state)
        return 0

    lax.fori_loop(0, pairs, pair_of_rows, 0)

    def total_of(k):
        return jnp.sum(rounded(points_s[k : k + 1, :]), axis=1, keepdims=True)

    planck_total, insol_total = total_of(0), total_of(1)

    def gathered(ref, l, g):
        base = g * ROWS * ROWS
        return sum(ref[l, pl.ds(base + k, ROWS, stride=ROWS), :] for k in range(ROWS))

    def source_of(l, g):
        return (1.0 + 0.25 * rounded(t_ref[l, g * ROWS : (g + 1) * ROWS])) * planck_total

    def finish(l, carry):
        after = jnp.minimum(l + 1, levels - 1)
        out = []
        for g in range(groups):
            down_in, up_out = carry[g]
            down_out = gathered(down_s, l, g) + source_of(l, g)
            up_in = source_of(after, g) - jnp.where(l == levels - 1, 0.0, gathered(up_s, after, g))
            heat_ref[l, g * ROWS : (g + 1) * ROWS] = (2.0 / gpoints) * (
                down_in - down_out + up_in - up_out
            )
            out.append((down_out, up_in))
        return tuple(out)

    begin = []
    for g in range(groups):
        lit = lit_s[g * ROWS : (g + 1) * ROWS]
        begin.append((lit * insol_total, source_of(0, g) - gathered(up_s, 0, g)))
    ends = unrolled(levels, 3, finish, tuple(begin))
    for g in range(groups):
        surface_s[g * ROWS : (g + 1) * ROWS] = ends[g][0] * (1.0 / gpoints)

    slots_ref[...] = jnp.zeros(slots_ref.shape, F32)

    def clear(h, _):
        taken_s[h] = 0
        return 0

    lax.fori_loop(0, slots_ref.shape[0] // capacity, clear, 0)

    def place(r, _):
        host = hosts_ref[r]
        k = taken_s[host]
        taken_s[host] = k + 1
        slots_ref[pl.ds(host * capacity + k, 1), :] = surface_s[pl.ds(r, 1), :]
        return 0

    lax.fori_loop(0, rows, place, 0)


VMEM_GRANT = 60 * 1024 * 1024


def radiate(hosts, daylight, host_count, capacity, t, q, c, mu, table, planck, insol, cond):
    levels, rows, width = t.shape
    gpoints = table.shape[1]
    padded = -(-gpoints // 16) * 16
    groups = rows // ROWS
    in_vmem = pl.BlockSpec(memory_space=pltpu.VMEM)
    two_rows = pltpu.VMEM((levels, padded, 2 * LANES), BF)
    per_tile = pltpu.VMEM((padded, LANES), BF)
    sums = pltpu.VMEM((levels, rows * ROWS, LANES), F32)
    return pl.pallas_call(
        functools.partial(column_kernel, gpoints, capacity),
        in_specs=[pl.BlockSpec(memory_space=pltpu.SMEM)] * 2 + [in_vmem] * 8,
        out_specs=[in_vmem, in_vmem],
        out_shape=[
            jax.ShapeDtypeStruct(t.shape, F32),
            jax.ShapeDtypeStruct((host_count * capacity, width), F32),
        ],
        scratch_shapes=[
            pltpu.VMEM((levels, padded, NODES), BF),
            per_tile,
            per_tile,
            per_tile,
            pltpu.VMEM((rows, width), F32),
            pltpu.VMEM((rows, width), F32),
            pltpu.VMEM((ROWS, -(-gpoints // LANES) * LANES), F32),
            pltpu.VMEM((groups, levels, NT, ROWS, LANES), F32),
            pltpu.VMEM((groups, levels, NQ * ROWS, LANES), F32),
            pltpu.VMEM((levels, rows, width), F32),
            two_rows,
            two_rows,
            sums,
            sums,
            pltpu.VMEM((rows, width), F32),
            pltpu.SMEM((host_count,), jnp.int32),
        ],
        compiler_params=pltpu.CompilerParams(vmem_limit_bytes=VMEM_GRANT),
        cost_estimate=pl.CostEstimate(
            flops=2 * levels * padded * 256 * rows * width,
            bytes_accessed=4 * 4 * levels * rows * width,
            transcendentals=2 * levels * padded * rows * width,
        ),
        name="columns",
    )(hosts, daylight, t, q, c, mu, table, planck[None], insol[None], cond[None])


def lines_of(levels):
    return -(-2 * levels // 32) * 32


def edge_kernel(t_ref, q_ref, out_ref):
    levels, rows, width = t_ref.shape
    lines = lines_of(levels)
    lane = lax.broadcasted_iota(jnp.int32, (rows, width), 1) // 2
    packed = jnp.zeros((rows, width), F32)
    for k, ref in enumerate((t_ref, q_ref)):
        for l in range(levels):
            n = k * levels + l
            v = ref[l]
            out_ref[n : n + 1, :] = v[:1]
            out_ref[lines + n : lines + n + 1, :] = v[rows - 1 :]
            packed = jnp.where(lane == n, pltpu.roll(v, 2 * n + 1, axis=1), packed)
    if lines > 2 * levels:
        rest = jnp.zeros((lines - 2 * levels, width), F32)
        out_ref[2 * levels : lines, :] = rest
        out_ref[lines + 2 * levels : 2 * lines, :] = rest
    out_ref[2 * lines :, :] = packed


def chunks(levels):
    count = max(n for n in range(1, 11) if levels % n == 0)
    return count, levels // count


def edges(t, q):
    levels, rows, width = t.shape
    return pl.pallas_call(
        edge_kernel,
        out_shape=jax.ShapeDtypeStruct((2 * lines_of(levels) + rows, width), F32),
        name="edges",
    )(t, q)


def stencil_kernel(
    levels, at_ref, t_ref, q_ref, heat_ref, west_ref, east_ref, south_ref, north_ref, t_out, q_out
):
    count, rows, width = t_ref.shape
    lane = lax.broadcasted_iota(jnp.int32, (rows, width), 1)
    row = lax.broadcasted_iota(jnp.int32, (rows, width), 0)

    def present(k, x):
        return jnp.where(at_ref[4 + k] != 0, x, 0.0)

    sides = jnp.where(
        lane % 2 == 0,
        present(1, pltpu.roll(east_ref[...], width - 1, axis=1)),
        present(0, pltpu.roll(west_ref[...], 1, axis=1)),
    )

    def smoothed(v, n):
        halo = pltpu.roll(sides, width - 1 - 2 * n, axis=1)
        west = jnp.where(lane == 0, halo, pltpu.roll(v, 1, axis=1))
        east = jnp.where(lane == width - 1, halo, pltpu.roll(v, width - 1, axis=1))
        below = present(2, south_ref[pl.ds(n, 1), :])
        above = present(3, north_ref[pl.ds(n, 1), :])
        south = jnp.where(row == 0, below, pltpu.roll(v, 1, axis=0))
        north = jnp.where(row == rows - 1, above, pltpu.roll(v, rows - 1, axis=0))
        return v + diffusion * (((north + south) + (east + west)) - 4.0 * v)

    for j in range(count):
        l = pl.program_id(0) * count + j
        t_out[j] = smoothed(t_ref[j], l) + heat_ref[j]
        q_out[j] = smoothed(q_ref[j], levels + l)


def diffuse(places, t, q, heating, packed):
    levels, rows, width = t.shape
    lines = lines_of(levels)
    count, steps = chunks(levels)
    block = pl.BlockSpec((count, rows, width), lambda i, at: (i, 0, 0))

    def part(which, height, place):
        return pl.BlockSpec((None, height, width), lambda i, at: (at[which], place, 0))

    out = jax.ShapeDtypeStruct(t.shape, F32)
    return pl.pallas_call(
        functools.partial(stencil_kernel, levels),
        grid_spec=pltpu.PrefetchScalarGridSpec(
            num_scalar_prefetch=1,
            grid=(steps,),
            in_specs=[
                block,
                block,
                block,
                part(0, rows, 2 * lines // rows),
                part(1, rows, 2 * lines // rows),
                part(2, lines, 1),
                part(3, lines, 0),
            ],
            out_specs=[block, block],
        ),
        out_shape=[out, out],
        cost_estimate=pl.CostEstimate(
            flops=200 * levels * rows * width * 8,
            bytes_accessed=5 * 4 * levels * rows * width,
            transcendentals=0,
        ),
        name="diffuse",
    )(places, t, q, heating, packed, packed, packed, packed)


def neighbour_places():
    x, y = lax.axis_index("gx"), lax.axis_index("gy")
    x_count, y_count = lax.axis_size("gx"), lax.axis_size("gy")
    places, exist = [], []
    for dx, dy in ((-1, 0), (1, 0), (0, -1), (0, 1)):
        there_x, there_y = x + dx, y + dy
        inside = jnp.logical_and(
            jnp.logical_and(there_x >= 0, there_x < x_count),
            jnp.logical_and(there_y >= 0, there_y < y_count),
        )
        places.append(jnp.where(inside, there_x * y_count + there_y, 0))
        exist.append(inside.astype(jnp.int32))
    return jnp.stack(places + exist).astype(jnp.int32)


def on_device(
    thermal_anomaly_grid,
    relative_moisture,
    overcast_share,
    sun_angle_projection,
    daylight_mask,
    radiator_owner_position,
    molecular_opacity_lookup,
    condensed_opacity_per_share,
    planck_emission_factor,
    insolation_quadrature_factor,
):
    host_count = lax.axis_size("gx")
    t, q = thermal_anomaly_grid, relative_moisture
    blocks = t.shape[1]
    capacity = max(2, (2 * blocks + host_count - 1) // host_count)

    packed = lax.all_gather(edges(t, q), ("gx", "gy"), axis=0)

    heating, sent = radiate(
        radiator_owner_position.reshape(blocks),
        daylight_mask.reshape(blocks),
        host_count,
        capacity,
        t,
        q,
        overcast_share,
        sun_angle_projection,
        molecular_opacity_lookup,
        planck_emission_factor,
        insolation_quadrature_factor,
        condensed_opacity_per_share,
    )
    slots = lax.all_to_all(
        sent.reshape(host_count, capacity, sent.shape[1]),
        "gx",
        split_axis=0,
        concat_axis=0,
        tiled=True,
    )
    t_next, q_next = diffuse(neighbour_places(), t, q, heating, packed)
    return t_next, q_next, slots[None, None]


def solution(mesh):
    placed = (
        P(None, "gy", "gx"),
        P(None, "gy", "gx"),
        P(None, "gy", "gx"),
        P("gy", "gx"),
        P("gx", "gy"),
        P("gx", "gy", None),
        P(),
        P(),
        P(),
        P(),
    )
    return jax.shard_map(
        on_device,
        mesh=mesh,
        in_specs=placed,
        out_specs=(P(None, "gy", "gx"), P(None, "gy", "gx"), P("gy", "gx", None, None, None)),
        check_vma=False,
    )
```

time: 101 us -> 99.8 us (0.988)
  the two profiles are of different devices: /device:TPU:27 before, /device:TPU:0 now
where the time goes in v2:
time: 99.8 us; the launch traced here: 99.5 us
  Pallas kernels  74.8 us (75%)
  between operations  14 us (14%)
  starting transfers between devices  5.21 us (5%)
  waiting for transfers between devices  4.2 us (4%)
  local copies, waits for them, and re-layouts  1.28 us (1%)
    pallas_call x1, Pallas kernels, radiate(): pl.pallas_call(functools.partial(column_kernel, gpoints, capacity), in_sp...  68.2 us
    all_to_all x1, starting transfers between devices, on_device(): lax.all_to_all(sent.reshape(host_count, capacity, sent.shape[1]), 'gx', s...  5.18 us
    pallas_call x1, Pallas kernels, diffuse(): pl.pallas_call(functools.partial(stencil_kernel, levels), grid_spec=pltpu...  4.4 us
    all_to_all x1, waiting for transfers between devices, on_device(): lax.all_to_all(sent.reshape(host_count, capacity, sent.shape[1]), 'gx', s...  4.18 us
    pallas_call x1, Pallas kernels, edges(): pl.pallas_call(edge_kernel, out_shape=jax.ShapeDtypeStruct((2 * lines_of(...  2.13 us
  transfers between devices with their start and end apart: 2, of which 1 were waited for; matrix products, arithmetic and copies ran while one was open for 1% of the time, Pallas kernels for 69%

profile of v2, /device:TPU:0, one launch (start us, length us, event | category | flops | bytes accessed | tf_op | source)
XLA Modules:
  0.0 99.5 jit_solution(2444224923240187570)
XLA Ops:
  7.2 0.0 all-gather.3.cloned.1.call-start
  7.2 2.1 %edges.1 = f32[160,128]{1,0:T(8,128)} custom-call(f32[30,32,128]{2,1,0:T(8,128)} %t_ref.5, f32[30,32,128]{2,1,0:T(8,128)} %q_ref.5), custom_call_target="tpu_custom_call" | custom-call | tf_op jit(solution)/shard_map/edges/pallas_call | solution.py:336
  9.3 0.0 all-gather.3.cloned.1.call-update
  9.4 68.2 %columns.1 = (f32[30,32,128]{2,1,0:T(8,128)}, f32[64,128]{1,0:T(8,128)}) custom-call(s32[32]{0:T(128)} %bitcast.25, s32[32]{0:T(128)} %bitcast.26, f32[30,32,128]{2,1,0:T(8,128)} %t_ref.5, f32[30,32,128]{2,1,0:T(8,128)} %q_ref.5, f32[30,32,128]{2,1,0:T(8,128)} %c_ref.1, f32[32,128]{1,0:T(8,128)} %mu_ref.1, bf16[30,140,128]{2,1,0:T(8,128)(2,1)} %table_ref.1, ...), custom_call_target="tpu_custom_call" | custom-call | flops 9059696640 | bytes 1966080 | tf_op jit(solution)/shard_map/columns/pallas_call | solution.py:270
  77.6 5.2 %all-to-all-start = ((f32[8,8,128]{2,1,0:T(8,128)}), f32[8,8,128]{2,1,0:T(8,128)S(1)}, u32[]{:S(2)}, u32[]{:S(2)}) async-start(f32[8,8,128]{2,1,0:T(8,128)} %bitcast.21), calls=%async_computation | async-start | bytes 65536 | tf_op jit(solution)/shard_map/all_to_all | solution.py:459
  82.8 0.7 stack.51.at_ref
  83.5 4.2 %all-to-all-done = f32[8,8,128]{2,1,0:T(8,128)S(1)} async-done(((f32[8,8,128]{2,1,0:T(8,128)}), f32[8,8,128]{2,1,0:T(8,128)S(1)}, u32[]{:S(2)}, u32[]{:S(2)}) %all-to-all-start) | async-done | bytes 32800 | tf_op jit(solution)/shard_map/all_to_all | solution.py:459
  87.6 0.0 all-gather.3.cloned.1.call-done
  87.6 4.4 %diffuse.1 = (f32[30,32,128]{2,1,0:T(8,128)}, f32[30,32,128]{2,1,0:T(8,128)}) custom-call(s32[8]{0:T(128)} %stack.51.at_ref, f32[30,32,128]{2,1,0:T(8,128)} %t_ref.5, f32[30,32,128]{2,1,0:T(8,128)} %q_ref.5, f32[30,32,128]{2,1,0:T(8,128)} %get-tuple-element.7.heat_ref, f32[32,160,128]{2,1,0:T(8,128)} %bitcast.16, f32[32,160,128]{2,1,0:T(8,128)} %bitcast.17, ...), custom_call_target="tpu_custom_call" | custom-call | flops 196608000 | bytes 2457600 | tf_op jit(solution)/shard_map/diffuse/pallas_call | solution.py:385
  92.0 0.6 copy.14
Async XLA Ops:
  7.2 80.5 %all-gather.3.cloned.1.call-start = ((), (), s32[]{:S(2)}) async-start(), calls=%async_computation.1 | async-start | bytes 2703360 | tf_op jit(solution)/shard_map/all_gather | solution.py:443
  77.6 10.0 %all-to-all-start = ((f32[8,8,128]{2,1,0:T(8,128)}), f32[8,8,128]{2,1,0:T(8,128)S(1)}, u32[]{:S(2)}, u32[]{:S(2)}) async-start(f32[8,8,128]{2,1,0:T(8,128)} %bitcast.21), calls=%async_computation | async-start | bytes 65536 | tf_op jit(solution)/shard_map/all_to_all | solution.py:459
Sparse Core Ops, SparseCore 0:
  11.4 60.7 all-gather.2

commit v3 on v2

--- a/solution.py
+++ b/solution.py
@@ -52,6 +52,9 @@
     cond_ref,
     heat_ref,
     slots_ref,
+    sides_ref,
+    low_ref,
+    high_ref,
     table_s,
     cond_s,
     planck_s,
@@ -60,7 +63,7 @@
     lit_s,
     points_s,
     th_s,
-    qh_s,
+    q_pos_s,
     dt_s,
     tr_s,
     beam_s,
@@ -75,6 +78,8 @@
     groups = rows // ROWS
     pairs = rows // 2
 
+    pack_edges(t_ref, q_ref, sides_ref, low_ref, high_ref)
+
     def prepare(l, _):
         layer = table_ref[l].astype(F32) * (-diffusivity * LOG2E)
         table_s[l] = jnp.concatenate(
@@ -97,10 +102,7 @@
 
     planck_s[...] = column(0).astype(BF)
     insol_s[...] = column(1).astype(BF)
-    cond = column(2) * (-diffusivity * LOG2E)
-    high = rounded(cond)
-    lane = lax.broadcasted_iota(jnp.int32, (padded, LANES), 1)
-    cond_s[...] = jnp.where(lane == 0, high, jnp.where(lane == 1, cond - high, 0.0)).astype(BF)
+    cond_s[...] = (column(2) * (-diffusivity * LOG2E)).astype(BF)
     inverse_s[...] = (1.0 / diffusivity) / rounded(mu_ref[...])
 
     def hats(l, _):
@@ -112,10 +114,7 @@
             q_pos = jnp.clip(rounded(q_ref[l, at]) * (NQ - 1.0), 0.0, NQ - 1.0)
             for i in range(NT):
                 th_s[g, l, i] = jnp.maximum(0.0, 1.0 - jnp.abs(t_pos - float(i)))
-            for j in range(NQ):
-                qh_s[g, l, j * ROWS : (j + 1) * ROWS] = jnp.maximum(
-                    0.0, 1.0 - jnp.abs(q_pos - float(j))
-                )
+            q_pos_s[l, at] = q_pos
             dt_s[l, at] = 0.25 * (t - rounded(t_ref[after, at]))
         return 0
 
@@ -130,7 +129,8 @@
 
     def weights(l, row):
         g, r = row // ROWS, row % ROWS
-        qh = qh_s[g, l, pl.ds(r, NQ, stride=ROWS), :]
+        node = lax.broadcasted_iota(jnp.int32, (NQ, LANES), 0).astype(F32)
+        qh = jnp.maximum(0.0, 1.0 - jnp.abs(spread(q_pos_s, (l,), row) - node))
         qh = jnp.concatenate([qh, qh], axis=0).astype(BF)
         parts = []
         for m in range(NT // 2):
@@ -138,8 +138,7 @@
                 [spread(th_s, (g, l, 2 * m), r), spread(th_s, (g, l, 2 * m + 1), r)], axis=0
             ).astype(BF)
             parts.append(pair * qh)
-        cloud = wide(c_ref, (l,), row)
-        return jnp.concatenate(parts + [cloud] * (NODES // 16), axis=0)
+        return jnp.concatenate(parts, axis=0)
 
     def both(make):
         return jnp.concatenate([make(0), make(1)], axis=1)
@@ -154,16 +153,17 @@
     def pair_of_rows(p, _):
         def transmit(l, _):
             rhs = both(lambda h: weights(l, 2 * p + h))
-            lhs = jnp.concatenate([table_s[l], cond_s[...]], axis=1)
-            depth = jnp.dot(lhs, rhs, preferred_element_type=F32)
+            depth = jnp.dot(table_s[l], rhs, preferred_element_type=F32)
+            cloud = both(lambda h: wide(c_ref, (l,), 2 * p + h))
             inverse = both(lambda h: wide(inverse_s, (), 2 * p + h))
             for k in range(tiles):
-                part = depth[tile(k)].astype(BF)
+                cond = cond_s[tile(k)]
+                part = depth[tile(k)].astype(BF) + jnp.concatenate([cond, cond], axis=1) * cloud
                 tr_s[l, tile(k)] = jnp.exp2(part)
                 beam_s[l, tile(k)] = jnp.exp2(part * inverse)
             return 0
 
-        unrolled(levels, 10, transmit, 0)
+        unrolled(levels, 30, transmit, 0)
 
         for h in range(2):
             row = 2 * p + h
@@ -175,9 +175,9 @@
                 step = wide(dt_s, (n,), row)
                 up_step = wide(dt_s, (jnp.maximum(m - 1, 0),), row)
                 down_total, up_total = 0.0, 0.0
-                for k in range(0, tiles, 2):
+                for k in range(0, tiles, 3):
                     down_part, up_part = 0.0, 0.0
-                    for j in range(k, min(k + 2, tiles)):
+                    for j in range(k, min(k + 3, tiles)):
                         planck = planck_s[tile(j)]
                         kept = tr_s[n, tile(j), lanes] * long[j]
                         short[j] = short[j] * beam_s[n, tile(j), lanes]
@@ -199,7 +199,7 @@
                 tuple(insol_s[tile(k)] * lit for k in range(tiles)),
                 (jnp.zeros((16, LANES), BF),) * tiles,
             )
-            unrolled(levels, 6, sweep, state)
+            unrolled(levels, 15, sweep, state)
         return 0
 
     lax.fori_loop(0, pairs, pair_of_rows, 0)
@@ -255,6 +255,22 @@
     lax.fori_loop(0, rows, place, 0)
 
 
+def pack_edges(t_ref, q_ref, sides_ref, low_ref, high_ref):
+    levels, rows, width = t_ref.shape
+    lane = lax.broadcasted_iota(jnp.int32, (rows, width), 1) // 2
+
+    def body(l, packed):
+        for k, ref in enumerate((t_ref, q_ref)):
+            n = k * levels + l
+            v = ref[l]
+            low_ref[pl.ds(n, 1), :] = v[:1]
+            high_ref[pl.ds(n, 1), :] = v[rows - 1 :]
+            packed = jnp.where(lane == n, pltpu.roll(v, 2 * n + 1, axis=1), packed)
+        return packed
+
+    sides_ref[...] = unrolled(levels, 6, body, jnp.zeros((rows, width), F32))
+
+
 VMEM_GRANT = 60 * 1024 * 1024
 
 
@@ -270,10 +286,13 @@
     return pl.pallas_call(
         functools.partial(column_kernel, gpoints, capacity),
         in_specs=[pl.BlockSpec(memory_space=pltpu.SMEM)] * 2 + [in_vmem] * 8,
-        out_specs=[in_vmem, in_vmem],
+        out_specs=[in_vmem] * 5,
         out_shape=[
             jax.ShapeDtypeStruct(t.shape, F32),
             jax.ShapeDtypeStruct((host_count * capacity, width), F32),
+            jax.ShapeDtypeStruct((rows, width), F32),
+            jax.ShapeDtypeStruct((2 * levels, width), F32),
+            jax.ShapeDtypeStruct((2 * levels, width), F32),
         ],
         scratch_shapes=[
             pltpu.VMEM((levels, padded, NODES), BF),
@@ -284,7 +303,7 @@
             pltpu.VMEM((rows, width), F32),
             pltpu.VMEM((ROWS, -(-gpoints // LANES) * LANES), F32),
             pltpu.VMEM((groups, levels, NT, ROWS, LANES), F32),
-            pltpu.VMEM((groups, levels, NQ * ROWS, LANES), F32),
+            pltpu.VMEM((levels, rows, width), F32),
             pltpu.VMEM((levels, rows, width), F32),
             two_rows,
             two_rows,
@@ -303,67 +322,30 @@
     )(hosts, daylight, t, q, c, mu, table, planck[None], insol[None], cond[None])
 
 
-def lines_of(levels):
-    return -(-2 * levels // 32) * 32
-
-
-def edge_kernel(t_ref, q_ref, out_ref):
-    levels, rows, width = t_ref.shape
-    lines = lines_of(levels)
-    lane = lax.broadcasted_iota(jnp.int32, (rows, width), 1) // 2
-    packed = jnp.zeros((rows, width), F32)
-    for k, ref in enumerate((t_ref, q_ref)):
-        for l in range(levels):
-            n = k * levels + l
-            v = ref[l]
-            out_ref[n : n + 1, :] = v[:1]
-            out_ref[lines + n : lines + n + 1, :] = v[rows - 1 :]
-            packed = jnp.where(lane == n, pltpu.roll(v, 2 * n + 1, axis=1), packed)
-    if lines > 2 * levels:
-        rest = jnp.zeros((lines - 2 * levels, width), F32)
-        out_ref[2 * levels : lines, :] = rest
-        out_ref[lines + 2 * levels : 2 * lines, :] = rest
-    out_ref[2 * lines :, :] = packed
-
-
 def chunks(levels):
     count = max(n for n in range(1, 11) if levels % n == 0)
     return count, levels // count
 
 
-def edges(t, q):
-    levels, rows, width = t.shape
-    return pl.pallas_call(
-        edge_kernel,
-        out_shape=jax.ShapeDtypeStruct((2 * lines_of(levels) + rows, width), F32),
-        name="edges",
-    )(t, q)
-
-
 def stencil_kernel(
-    levels, at_ref, t_ref, q_ref, heat_ref, west_ref, east_ref, south_ref, north_ref, t_out, q_out
+    levels, t_ref, q_ref, heat_ref, west_ref, east_ref, south_ref, north_ref, t_out, q_out
 ):
     count, rows, width = t_ref.shape
     lane = lax.broadcasted_iota(jnp.int32, (rows, width), 1)
     row = lax.broadcasted_iota(jnp.int32, (rows, width), 0)
 
-    def present(k, x):
-        return jnp.where(at_ref[4 + k] != 0, x, 0.0)
-
     sides = jnp.where(
         lane % 2 == 0,
-        present(1, pltpu.roll(east_ref[...], width - 1, axis=1)),
-        present(0, pltpu.roll(west_ref[...], 1, axis=1)),
+        pltpu.roll(east_ref[...], width - 1, axis=1),
+        pltpu.roll(west_ref[...], 1, axis=1),
     )
 
     def smoothed(v, n):
         halo = pltpu.roll(sides, width - 1 - 2 * n, axis=1)
         west = jnp.where(lane == 0, halo, pltpu.roll(v, 1, axis=1))
         east = jnp.where(lane == width - 1, halo, pltpu.roll(v, width - 1, axis=1))
-        below = present(2, south_ref[pl.ds(n, 1), :])
-        above = present(3, north_ref[pl.ds(n, 1), :])
-        south = jnp.where(row == 0, below, pltpu.roll(v, 1, axis=0))
-        north = jnp.where(row == rows - 1, above, pltpu.roll(v, rows - 1, axis=0))
+        south = jnp.where(row == 0, south_ref[pl.ds(n, 1), :], pltpu.roll(v, 1, axis=0))
+        north = jnp.where(row == rows - 1, north_ref[pl.ds(n, 1), :], pltpu.roll(v, rows - 1, axis=0))
         return v + diffusion * (((north + south) + (east + west)) - 4.0 * v)
 
     for j in range(count):
@@ -372,32 +354,20 @@
         q_out[j] = smoothed(q_ref[j], levels + l)
 
 
-def diffuse(places, t, q, heating, packed):
+def diffuse(t, q, heating, west, east, south, north):
     levels, rows, width = t.shape
-    lines = lines_of(levels)
     count, steps = chunks(levels)
-    block = pl.BlockSpec((count, rows, width), lambda i, at: (i, 0, 0))
-
-    def part(which, height, place):
-        return pl.BlockSpec((None, height, width), lambda i, at: (at[which], place, 0))
+    block = pl.BlockSpec((count, rows, width), lambda i: (i, 0, 0))
+
+    def whole(x):
+        return pl.BlockSpec(x.shape, lambda i: (0, 0))
 
     out = jax.ShapeDtypeStruct(t.shape, F32)
     return pl.pallas_call(
         functools.partial(stencil_kernel, levels),
-        grid_spec=pltpu.PrefetchScalarGridSpec(
-            num_scalar_prefetch=1,
-            grid=(steps,),
-            in_specs=[
-                block,
-                block,
-                block,
-                part(0, rows, 2 * lines // rows),
-                part(1, rows, 2 * lines // rows),
-                part(2, lines, 1),
-                part(3, lines, 0),
-            ],
-            out_specs=[block, block],
-        ),
+        grid=(steps,),
+        in_specs=[block, block, block, whole(west), whole(east), whole(south), whole(north)],
+        out_specs=[block, block],
         out_shape=[out, out],
         cost_estimate=pl.CostEstimate(
             flops=200 * levels * rows * width * 8,
@@ -405,22 +375,14 @@
             transcendentals=0,
         ),
         name="diffuse",
-    )(places, t, q, heating, packed, packed, packed, packed)
-
-
-def neighbour_places():
-    x, y = lax.axis_index("gx"), lax.axis_index("gy")
-    x_count, y_count = lax.axis_size("gx"), lax.axis_size("gy")
-    places, exist = [], []
-    for dx, dy in ((-1, 0), (1, 0), (0, -1), (0, 1)):
-        there_x, there_y = x + dx, y + dy
-        inside = jnp.logical_and(
-            jnp.logical_and(there_x >= 0, there_x < x_count),
-            jnp.logical_and(there_y >= 0, there_y < y_count),
-        )
-        places.append(jnp.where(inside, there_x * y_count + there_y, 0))
-        exist.append(inside.astype(jnp.int32))
-    return jnp.stack(places + exist).astype(jnp.int32)
+    )(t, q, heating, west, east, south, north)
+
+
+def neighbours(low_edge, high_edge, axis):
+    count = lax.axis_size(axis)
+    forward = [(i, i + 1) for i in range(count - 1)]
+    backward = [(target, source) for source, target in forward]
+    return lax.ppermute(high_edge, axis, forward), lax.ppermute(low_edge, axis, backward)
 
 
 def on_device(
@@ -440,9 +402,7 @@
     blocks = t.shape[1]
     capacity = max(2, (2 * blocks + host_count - 1) // host_count)
 
-    packed = lax.all_gather(edges(t, q), ("gx", "gy"), axis=0)
-
-    heating, sent = radiate(
+    heating, sent, sides, low, high = radiate(
         radiator_owner_position.reshape(blocks),
         daylight_mask.reshape(blocks),
         host_count,
@@ -463,7 +423,9 @@
         concat_axis=0,
         tiled=True,
     )
-    t_next, q_next = diffuse(neighbour_places(), t, q, heating, packed)
+    west, east = neighbours(sides, sides, "gx")
+    south, north = neighbours(low, high, "gy")
+    t_next, q_next = diffuse(t, q, heating, west, east, south, north)
     return t_next, q_next, slots[None, None]
 
 

time: 99.8 us -> 85 us (0.85)
  the two profiles are of different devices: /device:TPU:0 before, /device:TPU:20 now
where the time goes in v3:
time: 85 us; the launch traced here: 84.6 us
  Pallas kernels  63.4 us (75%)
  starting transfers between devices  15.1 us (18%)
  waiting for transfers between devices  4.22 us (5%)
  local copies, waits for them, and re-layouts  1.21 us (1%)
    pallas_call x1, Pallas kernels, radiate(): pl.pallas_call(functools.partial(column_kernel, gpoints, capacity), in_sp...  59.6 us
    ppermute x2, starting transfers between devices, neighbours(): lax.ppermute(low_edge, axis, backward)  5.47 us
    ppermute x2, starting transfers between devices, neighbours(): lax.ppermute(high_edge, axis, forward)  5.39 us
    all_to_all x1, starting transfers between devices, on_device(): lax.all_to_all(sent.reshape(host_count, capacity, sent.shape[1]), 'gx', s...  4.24 us
    ppermute x2, waiting for transfers between devices, neighbours(): lax.ppermute(high_edge, axis, forward)  4.21 us
    pallas_call x1, Pallas kernels, diffuse(): pl.pallas_call(functools.partial(stencil_kernel, levels), grid=(steps,),...  3.73 us
  transfers between devices with their start and end apart: 5, of which 1 were waited for; matrix products, arithmetic and copies ran while one was open for 0% of the time, Pallas kernels for 0%

profile of v3, /device:TPU:20, one launch (start us, length us, event | category | flops | bytes accessed | tf_op | source)
XLA Modules:
  0.0 84.6 jit_solution(4051110906015391025)
XLA Ops:
  0.6 59.6 %columns.1 = (f32[30,32,128]{2,1,0:T(8,128)}, f32[64,128]{1,0:T(8,128)}, f32[32,128]{1,0:T(8,128)}, f32[60,128]{1,0:T(8,128)}, f32[60,128]{1,0:T(8,128)}) custom-call(s32[32]{0:T(128)} %bitcast.12, s32[32]{0:T(128)} %bitcast.13, f32[30,32,128]{2,1,0:T(8,128)} %t_ref.3, f32[30,32,128]{2,1,0:T(8,128)} %q_ref.3, f32[30,32,128]{2,1,0:T(8,128)} %c_ref.1, ...), custom_call_target="tpu_custom_call" | custom-call | flops 9059696640 | bytes 1966080 | tf_op jit(solution)/shard_map/columns/pallas_call | solution.py:286
  60.3 3.5 %collective-permute-start.2 = (f32[60,128]{1,0:T(8,128)}, f32[60,128]{1,0:T(8,128)S(1)}, u32[]{:S(2)}, u32[]{:S(2)}) collective-permute-start(f32[60,128]{1,0:T(8,128)} %get-tuple-element.12), channel_id=1, source_target_pairs={{0,1},{1,2},{2,3},{4,5},{5,6},{6,7},{8,9},{9,10},{10,11},{12,13},{... | collective-permute-start | bytes 92168 | tf_op jit(solution)/shard_map/ppermute | solution.py:385
  63.7 2.4 %collective-permute-start.3 = (f32[60,128]{1,0:T(8,128)}, f32[60,128]{1,0:T(8,128)S(1)}, u32[]{:S(2)}, u32[]{:S(2)}) collective-permute-start(f32[60,128]{1,0:T(8,128)} %get-tuple-element.13), channel_id=1, source_target_pairs={{1,0},{2,1},{3,2},{5,4},{6,5},{7,6},{9,8},{10,9},{11,10},{13,12},{... | collective-permute-start | bytes 92168 | tf_op jit(solution)/shard_map/ppermute | solution.py:385
  66.1 4.2 %all-to-all-start = ((f32[8,8,128]{2,1,0:T(8,128)}), f32[8,8,128]{2,1,0:T(8,128)S(1)}, u32[]{:S(2)}, u32[]{:S(2)}) async-start(f32[8,8,128]{2,1,0:T(8,128)} %bitcast.8), calls=%async_computation | async-start | bytes 65536 | tf_op jit(solution)/shard_map/all_to_all | solution.py:419
  70.4 3.1 %collective-permute-start.1 = (f32[32,128]{1,0:T(8,128)}, f32[32,128]{1,0:T(8,128)S(1)}, u32[]{:S(2)}, u32[]{:S(2)}) collective-permute-start(f32[32,128]{1,0:T(8,128)} %get-tuple-element.11), channel_id=1, source_target_pairs={{4,0},{8,4},{12,8},{16,12},{20,16},{24,20},{28,24},{5,1},{9,5},{13... | collective-permute-start | bytes 49160 | tf_op jit(solution)/shard_map/ppermute | solution.py:385
  73.5 1.9 %collective-permute-start = (f32[32,128]{1,0:T(8,128)}, f32[32,128]{1,0:T(8,128)S(1)}, u32[]{:S(2)}, u32[]{:S(2)}) collective-permute-start(f32[32,128]{1,0:T(8,128)} %get-tuple-element.11), channel_id=1, source_target_pairs={{0,4},{4,8},{8,12},{12,16},{16,20},{20,24},{24,28},{1,5},{5,9},{9,... | collective-permute-start | bytes 49160 | tf_op jit(solution)/shard_map/ppermute | solution.py:385
  75.4 0.0 all-to-all-done
  75.4 0.0 collective-permute-done.1.east_ref
  75.4 0.0 copy-start.2
  75.4 4.2 %collective-permute-done.west_ref = f32[32,128]{1,0:T(8,128)S(1)} collective-permute-done((f32[32,128]{1,0:T(8,128)}, f32[32,128]{1,0:T(8,128)S(1)}, u32[]{:S(2)}, u32[]{:S(2)}) %collective-permute-start) | collective-permute-done | bytes 16416 | tf_op jit(solution)/shard_map/ppermute | solution.py:385
  79.6 0.0 copy-start.3
  79.6 0.0 collective-permute-done.2.south_ref
  79.6 0.0 copy-start
  79.6 0.0 collective-permute-done.3.north_ref
  79.7 0.0 copy-start.1
  79.7 0.0 copy-done.2
  79.7 0.6 copy-done.3
  80.2 0.0 copy-done
  80.3 0.0 copy-done.1
  80.3 3.7 %diffuse.1 = (f32[30,32,128]{2,1,0:T(8,128)}, f32[30,32,128]{2,1,0:T(8,128)}) custom-call(f32[30,32,128]{2,1,0:T(8,128)} %t_ref.3, f32[30,32,128]{2,1,0:T(8,128)} %q_ref.3, f32[30,32,128]{2,1,0:T(8,128)} %get-tuple-element.10.heat_ref, f32[32,128]{1,0:T(8,128)} %copy-done.3, f32[32,128]{1,0:T(8,128)} %copy-done.2, f32[60,128]{1,0:T(8,128)} %copy-done, ...), custom_call_target="tpu_custom_call" | custom-call | flops 196608000 | bytes 2457600 | tf_op jit(solution)/shard_map/diffuse/pallas_call | solution.py:366
  84.0 0.6 copy.14
Async XLA Ops:
  60.3 19.4 %collective-permute-start.2 = (f32[60,128]{1,0:T(8,128)}, f32[60,128]{1,0:T(8,128)S(1)}, u32[]{:S(2)}, u32[]{:S(2)}) collective-permute-start(f32[60,128]{1,0:T(8,128)} %get-tuple-element.12), channel_id=1, source_target_pairs={{0,1},{1,2},{2,3},{4,5},{5,6},{6,7},{8,9},{9,10},{10,11},{12,13},{... | collective-permute-start | bytes 92168 | tf_op jit(solution)/shard_map/ppermute | solution.py:385
  63.7 15.9 %collective-permute-start.3 = (f32[60,128]{1,0:T(8,128)}, f32[60,128]{1,0:T(8,128)S(1)}, u32[]{:S(2)}, u32[]{:S(2)}) collective-permute-start(f32[60,128]{1,0:T(8,128)} %get-tuple-element.13), channel_id=1, source_target_pairs={{1,0},{2,1},{3,2},{5,4},{6,5},{7,6},{9,8},{10,9},{11,10},{13,12},{... | collective-permute-start | bytes 92168 | tf_op jit(solution)/shard_map/ppermute | solution.py:385
  66.1 9.3 %all-to-all-start = ((f32[8,8,128]{2,1,0:T(8,128)}), f32[8,8,128]{2,1,0:T(8,128)S(1)}, u32[]{:S(2)}, u32[]{:S(2)}) async-start(f32[8,8,128]{2,1,0:T(8,128)} %bitcast.8), calls=%async_computation | async-start | bytes 65536 | tf_op jit(solution)/shard_map/all_to_all | solution.py:419
  70.4 5.1 %collective-permute-start.1 = (f32[32,128]{1,0:T(8,128)}, f32[32,128]{1,0:T(8,128)S(1)}, u32[]{:S(2)}, u32[]{:S(2)}) collective-permute-start(f32[32,128]{1,0:T(8,128)} %get-tuple-element.11), channel_id=1, source_target_pairs={{4,0},{8,4},{12,8},{16,12},{20,16},{24,20},{28,24},{5,1},{9,5},{13... | collective-permute-start | bytes 49160 | tf_op jit(solution)/shard_map/ppermute | solution.py:385
  73.5 6.2 %collective-permute-start = (f32[32,128]{1,0:T(8,128)}, f32[32,128]{1,0:T(8,128)S(1)}, u32[]{:S(2)}, u32[]{:S(2)}) collective-permute-start(f32[32,128]{1,0:T(8,128)} %get-tuple-element.11), channel_id=1, source_target_pairs={{0,4},{4,8},{8,12},{12,16},{16,20},{20,24},{24,28},{1,5},{5,9},{9,... | collective-permute-start | bytes 49160 | tf_op jit(solution)/shard_map/ppermute | solution.py:385
  75.4 4.2 %copy-start.2 = (f32[32,128]{1,0:T(8,128)}, f32[32,128]{1,0:T(8,128)S(1)}, u32[]{:S(2)}) copy-start(f32[32,128]{1,0:T(8,128)S(1)} %collective-permute-done.1.east_ref) | copy-start | bytes 49156
  79.6 0.6 copy-start.3
  79.6 0.6 copy-start
  79.7 0.6 copy-start.1

commit v4 on v3

--- a/solution.py
+++ b/solution.py
@@ -16,6 +16,7 @@
 
 diffusion = 0.2
 diffusivity = 1.66
+LAG = 1
 LOG2E = math.log2(math.e)
 
 BF = jnp.bfloat16
@@ -163,9 +164,7 @@
                 beam_s[l, tile(k)] = jnp.exp2(part * inverse)
             return 0
 
-        unrolled(levels, 30, transmit, 0)
-
-        for h in range(2):
+        def sweeps(h):
             row = 2 * p + h
             lanes = slice(h * LANES, (h + 1) * LANES)
 
@@ -173,7 +172,7 @@
                 long, short, rising = (list(part) for part in state)
                 m = levels - 1 - n
                 step = wide(dt_s, (n,), row)
-                up_step = wide(dt_s, (jnp.maximum(m - 1, 0),), row)
+                up_step = wide(dt_s, (max(m - 1, 0),), row)
                 down_total, up_total = 0.0, 0.0
                 for k in range(0, tiles, 3):
                     down_part, up_part = 0.0, 0.0
@@ -199,7 +198,22 @@
                 tuple(insol_s[tile(k)] * lit for k in range(tiles)),
                 (jnp.zeros((16, LANES), BF),) * tiles,
             )
-            unrolled(levels, 15, sweep, state)
+            return sweep, state
+
+        sweep, state = sweeps(0)
+        half = (levels + 1) // 2
+        for n in range(half + LAG):
+            if n < half:
+                transmit(n, 0)
+                if levels - 1 - n != n:
+                    transmit(levels - 1 - n, 0)
+            if n >= LAG:
+                state = sweep(n - LAG, state)
+        for n in range(half, levels):
+            state = sweep(n, state)
+        sweep, state = sweeps(1)
+        for n in range(levels):
+            state = sweep(n, state)
         return 0
 
     lax.fori_loop(0, pairs, pair_of_rows, 0)

time: 85 us -> 86.6 us (1.019)
  Pallas kernels: 63.4 us -> 65 us
    pallas_call x1, Pallas kernels: 59.6 us -> 61.3 us  [radiate(): pl.pallas_call(functools.partial(column_kernel, gpoints, capacity), in_sp...]
where the time goes in v4:
time: 86.6 us; the launch traced here: 86.2 us
  Pallas kernels  65 us (75%)
  starting transfers between devices  15.1 us (17%)
  waiting for transfers between devices  4.22 us (5%)
  local copies, waits for them, and re-layouts  1.21 us (1%)
    pallas_call x1, Pallas kernels, radiate(): pl.pallas_call(functools.partial(column_kernel, gpoints, capacity), in_sp...  61.3 us
    ppermute x2, starting transfers between devices, neighbours(): lax.ppermute(low_edge, axis, backward)  5.47 us
    ppermute x2, starting transfers between devices, neighbours(): lax.ppermute(high_edge, axis, forward)  5.39 us
    all_to_all x1, starting transfers between devices, on_device(): lax.all_to_all(sent.reshape(host_count, capacity, sent.shape[1]), 'gx', s...  4.24 us
    ppermute x2, waiting for transfers between devices, neighbours(): lax.ppermute(high_edge, axis, forward)  4.21 us
    pallas_call x1, Pallas kernels, diffuse(): pl.pallas_call(functools.partial(stencil_kernel, levels), grid=(steps,),...  3.73 us
  transfers between devices with their start and end apart: 5, of which 1 were waited for; matrix products, arithmetic and copies ran while one was open for 0% of the time, Pallas kernels for 0%

profile of v4, /device:TPU:20, one launch (start us, length us, event | category | flops | bytes accessed | tf_op | source)
XLA Modules:
  0.0 86.2 jit_solution(10203419237978421664)
XLA Ops:
  0.6 61.3 %columns.1 = (f32[30,32,128]{2,1,0:T(8,128)}, f32[64,128]{1,0:T(8,128)}, f32[32,128]{1,0:T(8,128)}, f32[60,128]{1,0:T(8,128)}, f32[60,128]{1,0:T(8,128)}) custom-call(s32[32]{0:T(128)} %bitcast.12, s32[32]{0:T(128)} %bitcast.13, f32[30,32,128]{2,1,0:T(8,128)} %t_ref.3, f32[30,32,128]{2,1,0:T(8,128)} %q_ref.3, f32[30,32,128]{2,1,0:T(8,128)} %c_ref.1, ...), custom_call_target="tpu_custom_call" | custom-call | flops 9059696640 | bytes 1966080 | tf_op jit(solution)/shard_map/columns/pallas_call | solution.py:300
  61.9 3.5 %collective-permute-start.2 = (f32[60,128]{1,0:T(8,128)}, f32[60,128]{1,0:T(8,128)S(1)}, u32[]{:S(2)}, u32[]{:S(2)}) collective-permute-start(f32[60,128]{1,0:T(8,128)} %get-tuple-element.12), channel_id=1, source_target_pairs={{0,1},{1,2},{2,3},{4,5},{5,6},{6,7},{8,9},{9,10},{10,11},{12,13},{... | collective-permute-start | bytes 92168 | tf_op jit(solution)/shard_map/ppermute | solution.py:399
  65.4 2.4 %collective-permute-start.3 = (f32[60,128]{1,0:T(8,128)}, f32[60,128]{1,0:T(8,128)S(1)}, u32[]{:S(2)}, u32[]{:S(2)}) collective-permute-start(f32[60,128]{1,0:T(8,128)} %get-tuple-element.13), channel_id=1, source_target_pairs={{1,0},{2,1},{3,2},{5,4},{6,5},{7,6},{9,8},{10,9},{11,10},{13,12},{... | collective-permute-start | bytes 92168 | tf_op jit(solution)/shard_map/ppermute | solution.py:399
  67.8 4.2 %all-to-all-start = ((f32[8,8,128]{2,1,0:T(8,128)}), f32[8,8,128]{2,1,0:T(8,128)S(1)}, u32[]{:S(2)}, u32[]{:S(2)}) async-start(f32[8,8,128]{2,1,0:T(8,128)} %bitcast.8), calls=%async_computation | async-start | bytes 65536 | tf_op jit(solution)/shard_map/all_to_all | solution.py:433
  72.0 3.1 %collective-permute-start.1 = (f32[32,128]{1,0:T(8,128)}, f32[32,128]{1,0:T(8,128)S(1)}, u32[]{:S(2)}, u32[]{:S(2)}) collective-permute-start(f32[32,128]{1,0:T(8,128)} %get-tuple-element.11), channel_id=1, source_target_pairs={{4,0},{8,4},{12,8},{16,12},{20,16},{24,20},{28,24},{5,1},{9,5},{13... | collective-permute-start | bytes 49160 | tf_op jit(solution)/shard_map/ppermute | solution.py:399
  75.1 1.9 %collective-permute-start = (f32[32,128]{1,0:T(8,128)}, f32[32,128]{1,0:T(8,128)S(1)}, u32[]{:S(2)}, u32[]{:S(2)}) collective-permute-start(f32[32,128]{1,0:T(8,128)} %get-tuple-element.11), channel_id=1, source_target_pairs={{0,4},{4,8},{8,12},{12,16},{16,20},{20,24},{24,28},{1,5},{5,9},{9,... | collective-permute-start | bytes 49160 | tf_op jit(solution)/shard_map/ppermute | solution.py:399
  77.0 0.0 all-to-all-done
  77.0 0.0 collective-permute-done.1.east_ref
  77.1 0.0 copy-start.2
  77.1 4.2 %collective-permute-done.west_ref = f32[32,128]{1,0:T(8,128)S(1)} collective-permute-done((f32[32,128]{1,0:T(8,128)}, f32[32,128]{1,0:T(8,128)S(1)}, u32[]{:S(2)}, u32[]{:S(2)}) %collective-permute-start) | collective-permute-done | bytes 16416 | tf_op jit(solution)/shard_map/ppermute | solution.py:399
  81.3 0.0 copy-start.3
  81.3 0.0 collective-permute-done.2.south_ref
  81.3 0.0 copy-start
  81.3 0.0 collective-permute-done.3.north_ref
  81.3 0.0 copy-start.1
  81.3 0.0 copy-done.2
  81.3 0.6 copy-done.3
  81.9 0.0 copy-done
  81.9 0.0 copy-done.1
  81.9 3.7 %diffuse.1 = (f32[30,32,128]{2,1,0:T(8,128)}, f32[30,32,128]{2,1,0:T(8,128)}) custom-call(f32[30,32,128]{2,1,0:T(8,128)} %t_ref.3, f32[30,32,128]{2,1,0:T(8,128)} %q_ref.3, f32[30,32,128]{2,1,0:T(8,128)} %get-tuple-element.10.heat_ref, f32[32,128]{1,0:T(8,128)} %copy-done.3, f32[32,128]{1,0:T(8,128)} %copy-done.2, f32[60,128]{1,0:T(8,128)} %copy-done, ...), custom_call_target="tpu_custom_call" | custom-call | flops 196608000 | bytes 2457600 | tf_op jit(solution)/shard_map/diffuse/pallas_call | solution.py:380
  85.6 0.6 copy.14
Async XLA Ops:
  61.9 19.4 %collective-permute-start.2 = (f32[60,128]{1,0:T(8,128)}, f32[60,128]{1,0:T(8,128)S(1)}, u32[]{:S(2)}, u32[]{:S(2)}) collective-permute-start(f32[60,128]{1,0:T(8,128)} %get-tuple-element.12), channel_id=1, source_target_pairs={{0,1},{1,2},{2,3},{4,5},{5,6},{6,7},{8,9},{9,10},{10,11},{12,13},{... | collective-permute-start | bytes 92168 | tf_op jit(solution)/shard_map/ppermute | solution.py:399
  65.4 15.9 %collective-permute-start.3 = (f32[60,128]{1,0:T(8,128)}, f32[60,128]{1,0:T(8,128)S(1)}, u32[]{:S(2)}, u32[]{:S(2)}) collective-permute-start(f32[60,128]{1,0:T(8,128)} %get-tuple-element.13), channel_id=1, source_target_pairs={{1,0},{2,1},{3,2},{5,4},{6,5},{7,6},{9,8},{10,9},{11,10},{13,12},{... | collective-permute-start | bytes 92168 | tf_op jit(solution)/shard_map/ppermute | solution.py:399
  67.8 9.3 %all-to-all-start = ((f32[8,8,128]{2,1,0:T(8,128)}), f32[8,8,128]{2,1,0:T(8,128)S(1)}, u32[]{:S(2)}, u32[]{:S(2)}) async-start(f32[8,8,128]{2,1,0:T(8,128)} %bitcast.8), calls=%async_computation | async-start | bytes 65536 | tf_op jit(solution)/shard_map/all_to_all | solution.py:433
  72.0 5.1 %collective-permute-start.1 = (f32[32,128]{1,0:T(8,128)}, f32[32,128]{1,0:T(8,128)S(1)}, u32[]{:S(2)}, u32[]{:S(2)}) collective-permute-start(f32[32,128]{1,0:T(8,128)} %get-tuple-element.11), channel_id=1, source_target_pairs={{4,0},{8,4},{12,8},{16,12},{20,16},{24,20},{28,24},{5,1},{9,5},{13... | collective-permute-start | bytes 49160 | tf_op jit(solution)/shard_map/ppermute | solution.py:399
  75.1 6.2 %collective-permute-start = (f32[32,128]{1,0:T(8,128)}, f32[32,128]{1,0:T(8,128)S(1)}, u32[]{:S(2)}, u32[]{:S(2)}) collective-permute-start(f32[32,128]{1,0:T(8,128)} %get-tuple-element.11), channel_id=1, source_target_pairs={{0,4},{4,8},{8,12},{12,16},{16,20},{20,24},{24,28},{1,5},{5,9},{9,... | collective-permute-start | bytes 49160 | tf_op jit(solution)/shard_map/ppermute | solution.py:399
  77.1 4.2 %copy-start.2 = (f32[32,128]{1,0:T(8,128)}, f32[32,128]{1,0:T(8,128)S(1)}, u32[]{:S(2)}) copy-start(f32[32,128]{1,0:T(8,128)S(1)} %collective-permute-done.1.east_ref) | copy-start | bytes 49156
  81.3 0.6 copy-start.3
  81.3 0.6 copy-start
  81.3 0.6 copy-start.1

commit v5 on v3

--- a/solution.py
+++ b/solution.py
@@ -165,41 +165,50 @@
 
         unrolled(levels, 30, transmit, 0)
 
-        for h in range(2):
-            row = 2 * p + h
-            lanes = slice(h * LANES, (h + 1) * LANES)
-
-            def sweep(n, state):
-                long, short, rising = (list(part) for part in state)
-                m = levels - 1 - n
-                step = wide(dt_s, (n,), row)
-                up_step = wide(dt_s, (jnp.maximum(m - 1, 0),), row)
-                down_total, up_total = 0.0, 0.0
-                for k in range(0, tiles, 3):
-                    down_part, up_part = 0.0, 0.0
-                    for j in range(k, min(k + 3, tiles)):
-                        planck = planck_s[tile(j)]
-                        kept = tr_s[n, tile(j), lanes] * long[j]
-                        short[j] = short[j] * beam_s[n, tile(j), lanes]
-                        long[j] = kept + planck * step
-                        risen = tr_s[m, tile(j), lanes] * rising[j]
-                        rising[j] = risen + planck * up_step
-                        down_part = kept + short[j] + down_part
-                        up_part = risen + up_part
-                    down_total = down_part.astype(F32) + down_total
-                    up_total = up_part.astype(F32) + up_total
-                put(down_s, n, row, down_total)
-                put(up_s, m, row, up_total)
-                return tuple(long), tuple(short), tuple(rising)
-
-            start = wide(t_ref, (0,), row) * jnp.asarray(-0.25, BF) - jnp.asarray(1.0, BF)
-            lit = wide(lit_s, (), row)
-            state = (
-                tuple(planck_s[tile(k)] * start for k in range(tiles)),
-                tuple(insol_s[tile(k)] * lit for k in range(tiles)),
-                (jnp.zeros((16, LANES), BF),) * tiles,
-            )
-            unrolled(levels, 15, sweep, state)
+        def pair_tile(ref, k):
+            one = ref[tile(k)]
+            return jnp.concatenate([one, one], axis=1)
+
+        def put_pair(ref, l, parts):
+            total = 0.0
+            for k in range(0, tiles, 3):
+                total = sum(parts[k + 1 : k + 3], parts[k]).astype(F32) + total
+            for h in range(2):
+                put(ref, l, 2 * p + h, total[:, h * LANES : (h + 1) * LANES])
+
+        def downward(l, state):
+            long, short = (list(part) for part in state)
+            step = both(lambda h: wide(dt_s, (l,), 2 * p + h))
+            parts = []
+            for k in range(tiles):
+                kept = tr_s[l, tile(k)] * long[k]
+                short[k] = short[k] * beam_s[l, tile(k)]
+                long[k] = kept + pair_tile(planck_s, k) * step
+                parts.append(kept + short[k])
+            put_pair(down_s, l, parts)
+            return tuple(long), tuple(short)
+
+        def upward(n, rising):
+            l = levels - 1 - n
+            step = both(lambda h: wide(dt_s, (jnp.maximum(l - 1, 0),), 2 * p + h))
+            rising = list(rising)
+            parts = []
+            for k in range(tiles):
+                risen = tr_s[l, tile(k)] * rising[k]
+                rising[k] = risen + pair_tile(planck_s, k) * step
+                parts.append(risen)
+            put_pair(up_s, l, parts)
+            return tuple(rising)
+
+        start = both(lambda h: wide(t_ref, (0,), 2 * p + h))
+        start = start * jnp.asarray(-0.25, BF) - jnp.asarray(1.0, BF)
+        lit = both(lambda h: wide(lit_s, (), 2 * p + h))
+        state = (
+            tuple(pair_tile(planck_s, k) * start for k in range(tiles)),
+            tuple(pair_tile(insol_s, k) * lit for k in range(tiles)),
+        )
+        unrolled(levels, 15, downward, state)
+        unrolled(levels, 15, upward, (jnp.zeros((16, 2 * LANES), BF),) * tiles)
         return 0
 
     lax.fori_loop(0, pairs, pair_of_rows, 0)

time: 85 us -> 74.2 us (0.87)
  Pallas kernels: 63.4 us -> 52.6 us
    pallas_call x1, Pallas kernels: 59.6 us -> 48.9 us  [radiate(): pl.pallas_call(functools.partial(column_kernel, gpoints, capacity), in_sp...]
where the time goes in v5:
time: 74.2 us; the launch traced here: 73.9 us
  Pallas kernels  52.6 us (71%)
  starting transfers between devices  15.1 us (20%)
  waiting for transfers between devices  4.22 us (6%)
  local copies, waits for them, and re-layouts  1.21 us (2%)
    pallas_call x1, Pallas kernels, radiate(): pl.pallas_call(functools.partial(column_kernel, gpoints, capacity), in_sp...  48.9 us
    ppermute x2, starting transfers between devices, neighbours(): lax.ppermute(low_edge, axis, backward)  5.47 us
    ppermute x2, starting transfers between devices, neighbours(): lax.ppermute(high_edge, axis, forward)  5.39 us
    all_to_all x1, starting transfers between devices, on_device(): lax.all_to_all(sent.reshape(host_count, capacity, sent.shape[1]), 'gx', s...  4.24 us
    ppermute x2, waiting for transfers between devices, neighbours(): lax.ppermute(high_edge, axis, forward)  4.21 us
    pallas_call x1, Pallas kernels, diffuse(): pl.pallas_call(functools.partial(stencil_kernel, levels), grid=(steps,),...  3.73 us
  transfers between devices with their start and end apart: 5, of which 1 were waited for; matrix products, arithmetic and copies ran while one was open for 0% of the time, Pallas kernels for 0%

profile of v5, /device:TPU:20, one launch (start us, length us, event | category | flops | bytes accessed | tf_op | source)
XLA Modules:
  0.0 73.9 jit_solution(7743450612614505023)
XLA Ops:
  0.6 48.9 %columns.1 = (f32[30,32,128]{2,1,0:T(8,128)}, f32[64,128]{1,0:T(8,128)}, f32[32,128]{1,0:T(8,128)}, f32[60,128]{1,0:T(8,128)}, f32[60,128]{1,0:T(8,128)}) custom-call(s32[32]{0:T(128)} %bitcast.12, s32[32]{0:T(128)} %bitcast.13, f32[30,32,128]{2,1,0:T(8,128)} %t_ref.3, f32[30,32,128]{2,1,0:T(8,128)} %q_ref.3, f32[30,32,128]{2,1,0:T(8,128)} %c_ref.1, ...), custom_call_target="tpu_custom_call" | custom-call | flops 9059696640 | bytes 1966080 | tf_op jit(solution)/shard_map/columns/pallas_call | solution.py:295
  49.5 3.5 %collective-permute-start.2 = (f32[60,128]{1,0:T(8,128)}, f32[60,128]{1,0:T(8,128)S(1)}, u32[]{:S(2)}, u32[]{:S(2)}) collective-permute-start(f32[60,128]{1,0:T(8,128)} %get-tuple-element.12), channel_id=1, source_target_pairs={{0,1},{1,2},{2,3},{4,5},{5,6},{6,7},{8,9},{9,10},{10,11},{12,13},{... | collective-permute-start | bytes 92168 | tf_op jit(solution)/shard_map/ppermute | solution.py:394
  53.0 2.4 %collective-permute-start.3 = (f32[60,128]{1,0:T(8,128)}, f32[60,128]{1,0:T(8,128)S(1)}, u32[]{:S(2)}, u32[]{:S(2)}) collective-permute-start(f32[60,128]{1,0:T(8,128)} %get-tuple-element.13), channel_id=1, source_target_pairs={{1,0},{2,1},{3,2},{5,4},{6,5},{7,6},{9,8},{10,9},{11,10},{13,12},{... | collective-permute-start | bytes 92168 | tf_op jit(solution)/shard_map/ppermute | solution.py:394
  55.4 4.2 %all-to-all-start = ((f32[8,8,128]{2,1,0:T(8,128)}), f32[8,8,128]{2,1,0:T(8,128)S(1)}, u32[]{:S(2)}, u32[]{:S(2)}) async-start(f32[8,8,128]{2,1,0:T(8,128)} %bitcast.8), calls=%async_computation | async-start | bytes 65536 | tf_op jit(solution)/shard_map/all_to_all | solution.py:428
  59.6 3.1 %collective-permute-start.1 = (f32[32,128]{1,0:T(8,128)}, f32[32,128]{1,0:T(8,128)S(1)}, u32[]{:S(2)}, u32[]{:S(2)}) collective-permute-start(f32[32,128]{1,0:T(8,128)} %get-tuple-element.11), channel_id=1, source_target_pairs={{4,0},{8,4},{12,8},{16,12},{20,16},{24,20},{28,24},{5,1},{9,5},{13... | collective-permute-start | bytes 49160 | tf_op jit(solution)/shard_map/ppermute | solution.py:394
  62.7 1.9 %collective-permute-start = (f32[32,128]{1,0:T(8,128)}, f32[32,128]{1,0:T(8,128)S(1)}, u32[]{:S(2)}, u32[]{:S(2)}) collective-permute-start(f32[32,128]{1,0:T(8,128)} %get-tuple-element.11), channel_id=1, source_target_pairs={{0,4},{4,8},{8,12},{12,16},{16,20},{20,24},{24,28},{1,5},{5,9},{9,... | collective-permute-start | bytes 49160 | tf_op jit(solution)/shard_map/ppermute | solution.py:394
  64.7 0.0 all-to-all-done
  64.7 0.0 collective-permute-done.1.east_ref
  64.7 0.0 copy-start.2
  64.7 4.2 %collective-permute-done.west_ref = f32[32,128]{1,0:T(8,128)S(1)} collective-permute-done((f32[32,128]{1,0:T(8,128)}, f32[32,128]{1,0:T(8,128)S(1)}, u32[]{:S(2)}, u32[]{:S(2)}) %collective-permute-start) | collective-permute-done | bytes 16416 | tf_op jit(solution)/shard_map/ppermute | solution.py:394
  68.9 0.0 copy-start.3
  68.9 0.0 collective-permute-done.2.south_ref
  68.9 0.0 copy-start
  68.9 0.0 collective-permute-done.3.north_ref
  68.9 0.0 copy-start.1
  68.9 0.0 copy-done.2
  68.9 0.6 copy-done.3
  69.5 0.0 copy-done
  69.5 0.0 copy-done.1
  69.5 3.7 %diffuse.1 = (f32[30,32,128]{2,1,0:T(8,128)}, f32[30,32,128]{2,1,0:T(8,128)}) custom-call(f32[30,32,128]{2,1,0:T(8,128)} %t_ref.3, f32[30,32,128]{2,1,0:T(8,128)} %q_ref.3, f32[30,32,128]{2,1,0:T(8,128)} %get-tuple-element.10.heat_ref, f32[32,128]{1,0:T(8,128)} %copy-done.3, f32[32,128]{1,0:T(8,128)} %copy-done.2, f32[60,128]{1,0:T(8,128)} %copy-done, ...), custom_call_target="tpu_custom_call" | custom-call | flops 196608000 | bytes 2457600 | tf_op jit(solution)/shard_map/diffuse/pallas_call | solution.py:375
  73.2 0.6 copy.14
Async XLA Ops:
  49.5 19.4 %collective-permute-start.2 = (f32[60,128]{1,0:T(8,128)}, f32[60,128]{1,0:T(8,128)S(1)}, u32[]{:S(2)}, u32[]{:S(2)}) collective-permute-start(f32[60,128]{1,0:T(8,128)} %get-tuple-element.12), channel_id=1, source_target_pairs={{0,1},{1,2},{2,3},{4,5},{5,6},{6,7},{8,9},{9,10},{10,11},{12,13},{... | collective-permute-start | bytes 92168 | tf_op jit(solution)/shard_map/ppermute | solution.py:394
  53.0 15.9 %collective-permute-start.3 = (f32[60,128]{1,0:T(8,128)}, f32[60,128]{1,0:T(8,128)S(1)}, u32[]{:S(2)}, u32[]{:S(2)}) collective-permute-start(f32[60,128]{1,0:T(8,128)} %get-tuple-element.13), channel_id=1, source_target_pairs={{1,0},{2,1},{3,2},{5,4},{6,5},{7,6},{9,8},{10,9},{11,10},{13,12},{... | collective-permute-start | bytes 92168 | tf_op jit(solution)/shard_map/ppermute | solution.py:394
  55.4 9.3 %all-to-all-start = ((f32[8,8,128]{2,1,0:T(8,128)}), f32[8,8,128]{2,1,0:T(8,128)S(1)}, u32[]{:S(2)}, u32[]{:S(2)}) async-start(f32[8,8,128]{2,1,0:T(8,128)} %bitcast.8), calls=%async_computation | async-start | bytes 65536 | tf_op jit(solution)/shard_map/all_to_all | solution.py:428
  59.6 5.1 %collective-permute-start.1 = (f32[32,128]{1,0:T(8,128)}, f32[32,128]{1,0:T(8,128)S(1)}, u32[]{:S(2)}, u32[]{:S(2)}) collective-permute-start(f32[32,128]{1,0:T(8,128)} %get-tuple-element.11), channel_id=1, source_target_pairs={{4,0},{8,4},{12,8},{16,12},{20,16},{24,20},{28,24},{5,1},{9,5},{13... | collective-permute-start | bytes 49160 | tf_op jit(solution)/shard_map/ppermute | solution.py:394
  62.7 6.2 %collective-permute-start = (f32[32,128]{1,0:T(8,128)}, f32[32,128]{1,0:T(8,128)S(1)}, u32[]{:S(2)}, u32[]{:S(2)}) collective-permute-start(f32[32,128]{1,0:T(8,128)} %get-tuple-element.11), channel_id=1, source_target_pairs={{0,4},{4,8},{8,12},{12,16},{16,20},{20,24},{24,28},{1,5},{5,9},{9,... | collective-permute-start | bytes 49160 | tf_op jit(solution)/shard_map/ppermute | solution.py:394
  64.7 4.2 %copy-start.2 = (f32[32,128]{1,0:T(8,128)}, f32[32,128]{1,0:T(8,128)S(1)}, u32[]{:S(2)}) copy-start(f32[32,128]{1,0:T(8,128)S(1)} %collective-permute-done.1.east_ref) | copy-start | bytes 49156
  68.9 0.6 copy-start.3
  68.9 0.6 copy-start
  68.9 0.6 copy-start.1
